TPU v7x, 128 devices: a whole 4x4x4 slice. The times are simulated.
128 devices in a mesh: blk: 16 (over x, z_hi, core), group: 8 (over z_lo, y).
Axes of the slice: x: 4, y: 4, z: 4 (z_hi: 2, z_lo: 2; z = z_hi * 2 + z_lo), core: 2. Of those that a mesh axis runs over, the one named last changes fastest.
Arguments:
- queries: bfloat16 [32768, 4096], P(('blk', 'group')), may hold values from -12 to 12
- keys: bfloat16 [32768, 512], P(('blk', 'group')), may hold values from -12 to 12
- values: bfloat16 [32768, 512], P(('blk', 'group')), may hold values from -6 to 6
- plan: int32 [32768], P(('blk', 'group')), may hold values from 0 to 32767, as said below
- doc_lengths: int32 [8, 4], P('group'), may hold values from 1 to 2048, 4096 in all within a row
Outputs:
- attended: bfloat16 [32768, 4096], P(('blk', 'group'))
Inputs may be any that keep to these rules, and one draw needn't show every extreme that they name: `plan`: A permutation of the slots; the tokens of one device go to at most 4 slots of any one device, and to exactly 4 slots of some device.
All inputs are finite; a program needn't handle non-finite values.
Results may differ from a plain program's by a relative error of at most 0.0091.
Values may be sent and summed in bfloat16 or wider, within the bound.
A program may use at most 64 MiB of HBM per device.

v0:
```python
import math

import jax
import jax.numpy as jnp
from jax import lax
from jax.sharding import PartitionSpec as P

QUERY_HEADS = 32
KEY_VALUE_HEADS = 4
HEAD_SIZE = 128


THETA = 500000.0


def shifted(block, axis, distance):
    devices = range(lax.axis_size(axis))
    route = [((i - distance) % len(devices), i) for i in devices]
    return lax.ppermute(block, axis, route)


def apply_rotary(entries, token_position, head_width):
    half_width = head_width // 2
    inv_freq = jnp.exp(
        -jnp.log(THETA) * (2.0 * jnp.arange(half_width, dtype=jnp.float32) / head_width)
    )
    angles = token_position.astype(jnp.float32)[:, None] * inv_freq[None, :]
    cosine = jnp.cos(angles)[:, None, :]
    sines = jnp.sin(angles)[:, None, :]
    front_half = entries[..., :half_width]
    back_half = entries[..., half_width:]
    return jnp.concatenate(
        [front_half * cosine - back_half * sines, back_half * cosine + front_half * sines], -1
    )


def locate(cycle_index, lengths):
    doc_ends = jnp.cumsum(lengths)
    document = jnp.sum((cycle_index[:, None] >= doc_ends[None, :]).astype(jnp.int32), 1)
    starts = doc_ends - lengths
    chosen = document[:, None] == jnp.arange(lengths.shape[0], dtype=jnp.int32)[None, :]
    doc_begin = jnp.sum(jnp.where(chosen, starts[None, :], 0), 1)
    return (document, cycle_index - doc_begin)


def folded_index(position, offset, rows, positions):
    half_rows = rows // 2
    return jnp.where(
        offset < half_rows,
        position * half_rows + offset,
        (2 * positions - 1 - position) * half_rows + offset - half_rows,
    )


def local(queries, keys, values, plan, doc_lengths):
    token_rows = queries.shape[0]
    head_groups = QUERY_HEADS // KEY_VALUE_HEADS
    blk_count = lax.axis_size("blk")
    grp_count = lax.axis_size("group")
    devices = blk_count * grp_count
    capacity = 2 * token_rows // devices
    slots_total = devices * capacity
    q_width = queries.shape[1]
    kv_width = 2 * keys.shape[1]
    target = plan // token_rows
    dest_hits = (target[:, None] == jnp.arange(devices, dtype=jnp.int32)[None, :]).astype(jnp.int32)
    dest_rank = jnp.sum((jnp.cumsum(dest_hits, 0) - 1) * dest_hits, 1)
    buffer_index = target * capacity + dest_rank
    source_row = (
        jnp.full((slots_total,), token_rows, jnp.int32)
        .at[buffer_index]
        .set(jnp.arange(token_rows, dtype=jnp.int32))
    )
    padded_q = jnp.concatenate([queries, jnp.zeros((1, q_width), queries.dtype)], 0)
    padded_kv = jnp.concatenate(
        [jnp.concatenate([keys, values], 1), jnp.zeros((1, kv_width), keys.dtype)], 0
    )
    padded_plan = jnp.concatenate([plan, jnp.full((1,), -1, jnp.int32)], 0)
    send_q = padded_q[source_row]
    send_kv = padded_kv[source_row]
    send_slot = padded_plan[source_row]
    got_q, got_kv, got_slot = (
        lax.all_to_all(
            send_q.reshape(devices, capacity, q_width),
            ("blk", "group"),
            split_axis=0,
            concat_axis=0,
            tiled=True,
        ),
        lax.all_to_all(
            send_kv.reshape(devices, capacity, kv_width),
            ("blk", "group"),
            split_axis=0,
            concat_axis=0,
            tiled=True,
        ),
        lax.all_to_all(
            send_slot.reshape(devices, capacity),
            ("blk", "group"),
            split_axis=0,
            concat_axis=0,
            tiled=True,
        ),
    )
    got_q = got_q.reshape(slots_total, q_width)
    got_kv = got_kv.reshape(slots_total, kv_width)
    got_slot = got_slot.reshape(slots_total)
    my_blk = lax.axis_index("blk")
    my_grp = lax.axis_index("group")
    slot_base = (my_blk * grp_count + my_grp) * token_rows
    is_valid = got_slot >= 0
    local_row = jnp.where(is_valid, got_slot - slot_base, token_rows)
    place_index = (
        jnp.zeros((token_rows,), jnp.int32)
        .at[local_row]
        .set(jnp.arange(slots_total, dtype=jnp.int32), mode="drop")
    )
    cycle_q = got_q[place_index]
    cycle_key_value = got_kv[place_index]
    lengths = doc_lengths[0]
    offsets = jnp.arange(token_rows, dtype=jnp.int32)
    cycle_index = folded_index(my_blk, offsets, token_rows, blk_count)
    document, token_position = locate(cycle_index, lengths)
    query_rotated = apply_rotary(
        cycle_q.astype(jnp.float32).reshape(token_rows, QUERY_HEADS, HEAD_SIZE),
        token_position,
        HEAD_SIZE,
    ).astype(jnp.bfloat16)
    query_rotated = query_rotated.reshape(token_rows, KEY_VALUE_HEADS, head_groups, HEAD_SIZE)
    key_rotated = apply_rotary(
        cycle_key_value[:, : KEY_VALUE_HEADS * HEAD_SIZE]
        .astype(jnp.float32)
        .reshape(token_rows, KEY_VALUE_HEADS, HEAD_SIZE),
        token_position,
        HEAD_SIZE,
    ).astype(jnp.bfloat16)
    key_value_block = jnp.concatenate(
        [
            key_rotated.reshape(token_rows, KEY_VALUE_HEADS * HEAD_SIZE),
            cycle_key_value[:, KEY_VALUE_HEADS * HEAD_SIZE :],
        ],
        1,
    )
    score_scale = 1.0 / math.sqrt(HEAD_SIZE)

    def absorb(att_state, present_value, source):
        key_index = folded_index(source, offsets, token_rows, blk_count)
        key_document, key_position = locate(key_index, lengths)
        allowed = (document[:, None] == key_document[None, :]) & (
            cycle_index[:, None] >= key_index[None, :]
        )
        running_max, row_total, accumulated = att_state
        key_portion = present_value[:, : KEY_VALUE_HEADS * HEAD_SIZE].reshape(
            token_rows, KEY_VALUE_HEADS, HEAD_SIZE
        )
        value_portion = present_value[:, KEY_VALUE_HEADS * HEAD_SIZE :].reshape(
            token_rows, KEY_VALUE_HEADS, HEAD_SIZE
        )
        scores = (
            jnp.einsum(
                "qhgd,khd->qhgk", query_rotated, key_portion, preferred_element_type=jnp.float32
            )
            * score_scale
        )
        scores = jnp.where(allowed[:, None, None, :], scores, -jnp.inf)
        new_max = jnp.maximum(running_max, jnp.max(scores, -1))
        safe_max = jnp.where(jnp.isfinite(new_max), new_max, 0.0)
        weights = jnp.exp(scores - safe_max[..., None])
        decay_factor = jnp.exp(running_max - safe_max)
        row_total = row_total * decay_factor + jnp.sum(weights, -1)
        accumulated = accumulated * decay_factor[..., None] + jnp.einsum(
            "qhgk,khd->qhgd",
            weights.astype(jnp.bfloat16),
            value_portion,
            preferred_element_type=jnp.float32,
        )
        return (new_max, row_total, accumulated)

    initial = (
        jnp.full((token_rows, KEY_VALUE_HEADS, head_groups), -jnp.inf, jnp.float32),
        jnp.zeros((token_rows, KEY_VALUE_HEADS, head_groups), jnp.float32),
        jnp.zeros((token_rows, KEY_VALUE_HEADS, head_groups, HEAD_SIZE), jnp.float32),
    )
    att_state = absorb(initial, key_value_block, my_blk)

    def cycle_step(step_num, loop_carry):
        inner_state, present_value = loop_carry
        present_value = shifted(present_value, "blk", 1)
        source = (my_blk - step_num) % blk_count
        return (absorb(inner_state, present_value, source), present_value)

    att_state, unused_block = lax.fori_loop(1, blk_count, cycle_step, (att_state, key_value_block))
    running_max, row_total, accumulated = att_state
    cycle_out = (
        (accumulated / row_total[..., None]).astype(jnp.bfloat16).reshape(token_rows, q_width)
    )
    padded_out = jnp.concatenate([cycle_out, jnp.zeros((1, q_width), cycle_out.dtype)], 0)
    outgoing = padded_out[local_row]
    returned = lax.all_to_all(
        outgoing.reshape(devices, capacity, q_width),
        ("blk", "group"),
        split_axis=0,
        concat_axis=0,
        tiled=True,
    )
    returned = returned.reshape(slots_total, q_width)
    return returned[buffer_index]


def solution(mesh):
    return jax.shard_map(
        local,
        mesh=mesh,
        in_specs=(
            P(("blk", "group"), None),
            P(("blk", "group"), None),
            P(("blk", "group"), None),
            P(("blk", "group")),
            P("group", None),
        ),
        out_specs=P(("blk", "group"), None),
        check_vma=False,
    )
```

profile of v0, /device:TPU:1, one launch (start us, length us, event | category | flops | bytes accessed | tf_op | source)
XLA Modules:
  0.0 573.7 jit_solution(17590410611207645843)
XLA Ops:
  4.8 3.5 gather_fusion.1
  9.1 11.5 %all-to-all-start.1 = ((s32[128,1,4]{2,1,0:T(1,128)}), s32[128,1,4]{2,1,0:T(1,128)S(1)}, u32[]{:S(2)}, u32[]{:S(2)}) async-start(s32[128,1,4]{2,1,0:T(1,128)} %bitcast.6), calls=%async_computation.1 | async-start | bytes 131072 | tf_op jit(solution)/shard_map/all_to_all | solution.py:97
  24.9 5.5 all-to-all-done.1
  31.1 4.3 all-to-all-start
  37.1 4.4 gather_fusion.3
  41.5 7.2 %reshape.370 = bf16[128,4,4096]{2,1,0:T(4,128)(2,1)} reshape(bf16[512,4096]{1,0:T(8,128)(2,1)} %gather_fusion.3) | data formatting | bytes 8388608 | tf_op jit(solution)/shard_map/reshape | solution.py:84
  48.7 6.1 %all-to-all-done = bf16[128,4,1024]{2,1,0:T(4,128)(2,1)S(1)} async-done(((bf16[128,4,1024]{2,1,0:T(4,128)(2,1)}), bf16[128,4,1024]{2,1,0:T(4,128)(2,1)S(1)}, u32[]{:S(2)}, u32[]{:S(2)}) %all-to-all-start) | async-done | bytes 1048608 | tf_op jit(solution)/shard_map/all_to_all | solution.py:90
  54.8 5.6 all-to-all-start.2
  67.7 47.2 %all-to-all-done.2 = bf16[128,4,4096]{2,1,0:T(4,128)(2,1)} async-done(((bf16[128,4,4096]{2,1,0:T(4,128)(2,1)}), bf16[128,4,4096]{2,1,0:T(4,128)(2,1)}, u32[]{:S(2)}, u32[]{:S(2)}) %all-to-all-start.2) | async-done | bytes 4194336 | tf_op jit(solution)/shard_map/all_to_all | solution.py:83
  114.9 7.1 %reshape.371 = bf16[512,4096]{1,0:T(8,128)(2,1)} reshape(bf16[128,4,4096]{2,1,0:T(4,128)(2,1)} %all-to-all-done.2) | data formatting | bytes 8388608 | tf_op jit(solution)/shard_map/reshape | solution.py:105
  122.0 6.6 %gather_fusion.4 = bf16[256,4096]{1,0:T(8,128)(2,1)S(1)} fusion(bf16[512,4096]{1,0:T(8,128)(2,1)} %reshape.371, s32[1024]{0:T(1024)S(1)} %pad_clamp_fusion.2), kind=kCustom, calls=%fused_computation.4 | custom fusion | bytes 4195328 | tf_op jit(solution)/shard_map/gather | solution.py:118
  131.4 4.9 subtract_convert_fusion
  136.3 13.4 %pad_maximum_fusion = bf16[256,4,8,128]{3,0,2,1:T(8,128)(2,1)S(1)} fusion(bf16[256,4,8,64]{3,0,2,1:T(8,128)(2,1)S(1)} %bitcast.111, bf16[256,4,8,64]{3,0,2,1:T(8,128)(2,1)S(1)} %bitcast.110), kind=kLoop, calls=%fused_computation.51 | loop fusion | flops 4194304 | bytes 4194304 | tf_op jit(solution)/shard_map/concatenate | solution.py:32
  152.8 4.3 bitcast_add_fusion.1
  157.1 5.3 copy.63
  162.5 309.0 %while.23 = (s32[]{:T(128)}, f32[256,4,8]{0,2,1:T(8,128)S(1)}, f32[256,4,8]{0,2,1:T(8,128)S(1)}, f32[256,4,8,128]{3,0,2,1:T(8,128)}, bf16[256,1024]{0,1:T(8,128)...) while((s32[]{:T(128)}, f32[256,4,8]{0,2,1:T(8,128)S(1)}, ...), condition=%wide.region_15.16_spmd.clone.clone, body=%wide.region_11.15_spmd.clone.clone.sunk | while | flops 1099158528 | bytes 74752440 | solution.py:192
  162.7 5.9 %collective-permute-done = bf16[256,1024]{0,1:T(8,128)(2,1)S(1)} collective-permute-done((bf16[256,1024]{0,1:T(8,128)(2,1)S(1)}, bf16[256,1024]{0,1:T(8,128)(2,1)S(1)}, u32[]{:S(2)}, u32[]{:S(2)}) %collective-permute-start) | collective-permute-done | bytes 524320 | tf_op jit(solution)/shard_map/while/body/eval_jaxpr/ppermute | solution.py:19
  172.3 3.4 bitcast_add_fusion.3
  177.7 4.0 collective-permute-start
  181.9 5.9 %collective-permute-done = bf16[256,1024]{0,1:T(8,128)(2,1)S(1)} collective-permute-done((bf16[256,1024]{0,1:T(8,128)(2,1)S(1)}, bf16[256,1024]{0,1:T(8,128)(2,1)S(1)}, u32[]{:S(2)}, u32[]{:S(2)}) %collective-permute-start) | collective-permute-done | bytes 524320 | tf_op jit(solution)/shard_map/while/body/eval_jaxpr/ppermute | solution.py:19
  191.5 3.4 bitcast_add_fusion.3
  196.9 4.0 collective-permute-start
  201.1 5.9 %collective-permute-done = bf16[256,1024]{0,1:T(8,128)(2,1)S(1)} collective-permute-done((bf16[256,1024]{0,1:T(8,128)(2,1)S(1)}, bf16[256,1024]{0,1:T(8,128)(2,1)S(1)}, u32[]{:S(2)}, u32[]{:S(2)}) %collective-permute-start) | collective-permute-done | bytes 524320 | tf_op jit(solution)/shard_map/while/body/eval_jaxpr/ppermute | solution.py:19
  210.8 3.4 bitcast_add_fusion.3
  216.1 4.0 collective-permute-start
  220.3 7.5 %collective-permute-done = bf16[256,1024]{0,1:T(8,128)(2,1)S(1)} collective-permute-done((bf16[256,1024]{0,1:T(8,128)(2,1)S(1)}, bf16[256,1024]{0,1:T(8,128)(2,1)S(1)}, u32[]{:S(2)}, u32[]{:S(2)}) %collective-permute-start) | collective-permute-done | bytes 524320 | tf_op jit(solution)/shard_map/while/body/eval_jaxpr/ppermute | solution.py:19
  231.6 3.4 bitcast_add_fusion.3
  239.6 9.6 %collective-permute-done = bf16[256,1024]{0,1:T(8,128)(2,1)S(1)} collective-permute-done((bf16[256,1024]{0,1:T(8,128)(2,1)S(1)}, bf16[256,1024]{0,1:T(8,128)(2,1)S(1)}, u32[]{:S(2)}, u32[]{:S(2)}) %collective-permute-start) | collective-permute-done | bytes 524320 | tf_op jit(solution)/shard_map/while/body/eval_jaxpr/ppermute | solution.py:19
  252.9 3.4 bitcast_add_fusion.3
  258.8 11.7 %collective-permute-done = bf16[256,1024]{0,1:T(8,128)(2,1)S(1)} collective-permute-done((bf16[256,1024]{0,1:T(8,128)(2,1)S(1)}, bf16[256,1024]{0,1:T(8,128)(2,1)S(1)}, u32[]{:S(2)}, u32[]{:S(2)}) %collective-permute-start) | collective-permute-done | bytes 524320 | tf_op jit(solution)/shard_map/while/body/eval_jaxpr/ppermute | solution.py:19
  274.2 3.4 bitcast_add_fusion.3
  279.8 12.0 %collective-permute-done = bf16[256,1024]{0,1:T(8,128)(2,1)S(1)} collective-permute-done((bf16[256,1024]{0,1:T(8,128)(2,1)S(1)}, bf16[256,1024]{0,1:T(8,128)(2,1)S(1)}, u32[]{:S(2)}, u32[]{:S(2)}) %collective-permute-start) | collective-permute-done | bytes 524320 | tf_op jit(solution)/shard_map/while/body/eval_jaxpr/ppermute | solution.py:19
  301.2 12.0 %collective-permute-done = bf16[256,1024]{0,1:T(8,128)(2,1)S(1)} collective-permute-done((bf16[256,1024]{0,1:T(8,128)(2,1)S(1)}, bf16[256,1024]{0,1:T(8,128)(2,1)S(1)}, u32[]{:S(2)}, u32[]{:S(2)}) %collective-permute-start) | collective-permute-done | bytes 524320 | tf_op jit(solution)/shard_map/while/body/eval_jaxpr/ppermute | solution.py:19
  316.9 3.4 bitcast_add_fusion.3
  322.5 12.0 %collective-permute-done = bf16[256,1024]{0,1:T(8,128)(2,1)S(1)} collective-permute-done((bf16[256,1024]{0,1:T(8,128)(2,1)S(1)}, bf16[256,1024]{0,1:T(8,128)(2,1)S(1)}, u32[]{:S(2)}, u32[]{:S(2)}) %collective-permute-start) | collective-permute-done | bytes 524320 | tf_op jit(solution)/shard_map/while/body/eval_jaxpr/ppermute | solution.py:19
  338.2 3.4 bitcast_add_fusion.3
  343.8 12.0 %collective-permute-done = bf16[256,1024]{0,1:T(8,128)(2,1)S(1)} collective-permute-done((bf16[256,1024]{0,1:T(8,128)(2,1)S(1)}, bf16[256,1024]{0,1:T(8,128)(2,1)S(1)}, u32[]{:S(2)}, u32[]{:S(2)}) %collective-permute-start) | collective-permute-done | bytes 524320 | tf_op jit(solution)/shard_map/while/body/eval_jaxpr/ppermute | solution.py:19
  365.1 12.0 %collective-permute-done = bf16[256,1024]{0,1:T(8,128)(2,1)S(1)} collective-permute-done((bf16[256,1024]{0,1:T(8,128)(2,1)S(1)}, bf16[256,1024]{0,1:T(8,128)(2,1)S(1)}, u32[]{:S(2)}, u32[]{:S(2)}) %collective-permute-start) | collective-permute-done | bytes 524320 | tf_op jit(solution)/shard_map/while/body/eval_jaxpr/ppermute | solution.py:19
  386.5 12.0 %collective-permute-done = bf16[256,1024]{0,1:T(8,128)(2,1)S(1)} collective-permute-done((bf16[256,1024]{0,1:T(8,128)(2,1)S(1)}, bf16[256,1024]{0,1:T(8,128)(2,1)S(1)}, u32[]{:S(2)}, u32[]{:S(2)}) %collective-permute-start) | collective-permute-done | bytes 524320 | tf_op jit(solution)/shard_map/while/body/eval_jaxpr/ppermute | solution.py:19
  407.8 12.0 %collective-permute-done = bf16[256,1024]{0,1:T(8,128)(2,1)S(1)} collective-permute-done((bf16[256,1024]{0,1:T(8,128)(2,1)S(1)}, bf16[256,1024]{0,1:T(8,128)(2,1)S(1)}, u32[]{:S(2)}, u32[]{:S(2)}) %collective-permute-start) | collective-permute-done | bytes 524320 | tf_op jit(solution)/shard_map/while/body/eval_jaxpr/ppermute | solution.py:19
  429.1 12.0 %collective-permute-done = bf16[256,1024]{0,1:T(8,128)(2,1)S(1)} collective-permute-done((bf16[256,1024]{0,1:T(8,128)(2,1)S(1)}, bf16[256,1024]{0,1:T(8,128)(2,1)S(1)}, u32[]{:S(2)}, u32[]{:S(2)}) %collective-permute-start) | collective-permute-done | bytes 524320 | tf_op jit(solution)/shard_map/while/body/eval_jaxpr/ppermute | solution.py:19
  450.4 12.0 %collective-permute-done = bf16[256,1024]{0,1:T(8,128)(2,1)S(1)} collective-permute-done((bf16[256,1024]{0,1:T(8,128)(2,1)S(1)}, bf16[256,1024]{0,1:T(8,128)(2,1)S(1)}, u32[]{:S(2)}, u32[]{:S(2)}) %collective-permute-start) | collective-permute-done | bytes 524320 | tf_op jit(solution)/shard_map/while/body/eval_jaxpr/ppermute | solution.py:19
  476.9 4.4 gather_fusion.5
  481.3 7.2 %reshape.374 = bf16[128,4,4096]{2,1,0:T(4,128)(2,1)} reshape(bf16[512,4096]{1,0:T(8,128)(2,1)} %gather_fusion.5) | data formatting | bytes 8388608 | tf_op jit(solution)/shard_map/reshape | solution.py:200
  488.5 15.9 %all-to-all-start.3 = ((bf16[128,4,4096]{2,1,0:T(4,128)(2,1)}), bf16[128,4,4096]{2,1,0:T(4,128)(2,1)}, u32[]{:S(2)}, u32[]{:S(2)}) async-start(bf16[128,4,4096]{2,1,0:T(4,128)(2,1)} %reshape.374), calls=%async_computation.3 | async-start | bytes 8388608 | tf_op jit(solution)/shard_map/all_to_all | solution.py:199
  504.4 54.2 %all-to-all-done.3 = bf16[128,4,4096]{2,1,0:T(4,128)(2,1)} async-done(((bf16[128,4,4096]{2,1,0:T(4,128)(2,1)}), bf16[128,4,4096]{2,1,0:T(4,128)(2,1)}, u32[]{:S(2)}, u32[]{:S(2)}) %all-to-all-start.3) | async-done | bytes 4194336 | tf_op jit(solution)/shard_map/all_to_all | solution.py:199
  558.6 6.9 %reshape.375 = bf16[512,4096]{1,0:T(8,128)(2,1)} reshape(bf16[128,4,4096]{2,1,0:T(4,128)(2,1)} %all-to-all-done.3) | data formatting | bytes 8388608 | tf_op jit(solution)/shard_map/reshape | solution.py:206
  565.5 7.9 %gather_fusion.6 = bf16[256,4096]{1,0:T(8,128)(2,1)} fusion(bf16[512,4096]{1,0:T(8,128)(2,1)} %reshape.375, s32[1024]{0:T(1024)S(1)} %pad_clamp_fusion), kind=kCustom, calls=%fused_computation.6 | custom fusion | bytes 4195328 | tf_op jit(solution)/shard_map/gather | solution.py:207
  (304 shorter events, 144.5 us)
Async XLA Ops:
  9.1 21.4 %all-to-all-start.1 = ((s32[128,1,4]{2,1,0:T(1,128)}), s32[128,1,4]{2,1,0:T(1,128)S(1)}, u32[]{:S(2)}, u32[]{:S(2)}) async-start(s32[128,1,4]{2,1,0:T(1,128)} %bitcast.6), calls=%async_computation.1 | async-start | bytes 131072 | tf_op jit(solution)/shard_map/all_to_all | solution.py:97
  31.1 23.7 %all-to-all-start = ((bf16[128,4,1024]{2,1,0:T(4,128)(2,1)}), bf16[128,4,1024]{2,1,0:T(4,128)(2,1)S(1)}, u32[]{:S(2)}, u32[]{:S(2)}) async-start(bf16[128,4,1024]{2,1,0:T(4,128)(2,1)} %reshape.365), calls=%async_computation | async-start | bytes 2097152 | tf_op jit(solution)/shard_map/all_to_all | solution.py:90
  48.7 11.7 %copy-start.6 = (s32[1,4]{1,0:T(1,128)S(1)}, s32[1,4]{1,0:T(1,128)}, u32[]{:S(2)}) copy-start(s32[1,4]{1,0:T(1,128)} %param.11) | copy-start | bytes 52
  48.7 12.9 %copy-start.3 = (s32[128,1,4]{2,1,0:T(1,128)S(1)}, s32[128,1,4]{2,1,0:T(1,128)}, u32[]{:S(2)}) copy-start(s32[128,1,4]{2,1,0:T(1,128)} %copy-done.2) | copy-start | bytes 6148
  54.8 60.1 %all-to-all-start.2 = ((bf16[128,4,4096]{2,1,0:T(4,128)(2,1)}), bf16[128,4,4096]{2,1,0:T(4,128)(2,1)}, u32[]{:S(2)}, u32[]{:S(2)}) async-start(bf16[128,4,4096]{2,1,0:T(4,128)(2,1)} %reshape.370), calls=%async_computation.2 | async-start | bytes 8388608 | tf_op jit(solution)/shard_map/all_to_all | solution.py:83
  162.5 6.1 %collective-permute-start = (bf16[256,1024]{0,1:T(8,128)(2,1)S(1)}, bf16[256,1024]{0,1:T(8,128)(2,1)S(1)}, u32[]{:S(2)}, u32[]{:S(2)}) collective-permute-start(bf16[256,1024]{0,1:T(8,128)(2,1)S(1)} %get-tuple-element.538), channel_id=1, source_target_pairs={{120,0},{0,8},{8,16},{16,24},{24,32},{32,40},{40,48},{48,56},{56,6... | collective-permute-start | bytes 1572872 | tf_op jit(solution)/shard_map/while/body/eval_jaxpr/ppermute | solution.py:19
  170.2 2.2 copy-start
  175.8 1.9 copy-start.1
  177.7 10.1 %collective-permute-start = (bf16[256,1024]{0,1:T(8,128)(2,1)S(1)}, bf16[256,1024]{0,1:T(8,128)(2,1)S(1)}, u32[]{:S(2)}, u32[]{:S(2)}) collective-permute-start(bf16[256,1024]{0,1:T(8,128)(2,1)S(1)} %get-tuple-element.538), channel_id=1, source_target_pairs={{120,0},{0,8},{8,16},{16,24},{24,32},{32,40},{40,48},{48,56},{56,6... | collective-permute-start | bytes 1572872 | tf_op jit(solution)/shard_map/while/body/eval_jaxpr/ppermute | solution.py:19
  189.3 2.2 copy-start
  195.0 1.9 copy-start.1
  196.9 10.1 %collective-permute-start = (bf16[256,1024]{0,1:T(8,128)(2,1)S(1)}, bf16[256,1024]{0,1:T(8,128)(2,1)S(1)}, u32[]{:S(2)}, u32[]{:S(2)}) collective-permute-start(bf16[256,1024]{0,1:T(8,128)(2,1)S(1)} %get-tuple-element.538), channel_id=1, source_target_pairs={{120,0},{0,8},{8,16},{16,24},{24,32},{32,40},{40,48},{48,56},{56,6... | collective-permute-start | bytes 1572872 | tf_op jit(solution)/shard_map/while/body/eval_jaxpr/ppermute | solution.py:19
  208.6 2.2 copy-start
  214.2 1.9 copy-start.1
  216.1 11.7 %collective-permute-start = (bf16[256,1024]{0,1:T(8,128)(2,1)S(1)}, bf16[256,1024]{0,1:T(8,128)(2,1)S(1)}, u32[]{:S(2)}, u32[]{:S(2)}) collective-permute-start(bf16[256,1024]{0,1:T(8,128)(2,1)S(1)} %get-tuple-element.538), channel_id=1, source_target_pairs={{120,0},{0,8},{8,16},{16,24},{24,32},{32,40},{40,48},{48,56},{56,6... | collective-permute-start | bytes 1572872 | tf_op jit(solution)/shard_map/while/body/eval_jaxpr/ppermute | solution.py:19
  229.4 2.2 copy-start
  235.0 1.9 copy-start.1
  237.0 12.2 %collective-permute-start = (bf16[256,1024]{0,1:T(8,128)(2,1)S(1)}, bf16[256,1024]{0,1:T(8,128)(2,1)S(1)}, u32[]{:S(2)}, u32[]{:S(2)}) collective-permute-start(bf16[256,1024]{0,1:T(8,128)(2,1)S(1)} %get-tuple-element.538), channel_id=1, source_target_pairs={{120,0},{0,8},{8,16},{16,24},{24,32},{32,40},{40,48},{48,56},{56,6... | collective-permute-start | bytes 1572872 | tf_op jit(solution)/shard_map/while/body/eval_jaxpr/ppermute | solution.py:19
  250.7 2.2 copy-start
  256.4 1.9 copy-start.1
  258.3 12.2 %collective-permute-start = (bf16[256,1024]{0,1:T(8,128)(2,1)S(1)}, bf16[256,1024]{0,1:T(8,128)(2,1)S(1)}, u32[]{:S(2)}, u32[]{:S(2)}) collective-permute-start(bf16[256,1024]{0,1:T(8,128)(2,1)S(1)} %get-tuple-element.538), channel_id=1, source_target_pairs={{120,0},{0,8},{8,16},{16,24},{24,32},{32,40},{40,48},{48,56},{56,6... | collective-permute-start | bytes 1572872 | tf_op jit(solution)/shard_map/while/body/eval_jaxpr/ppermute | solution.py:19
  272.0 2.2 copy-start
  277.7 1.9 copy-start.1
  279.6 12.2 %collective-permute-start = (bf16[256,1024]{0,1:T(8,128)(2,1)S(1)}, bf16[256,1024]{0,1:T(8,128)(2,1)S(1)}, u32[]{:S(2)}, u32[]{:S(2)}) collective-permute-start(bf16[256,1024]{0,1:T(8,128)(2,1)S(1)} %get-tuple-element.538), channel_id=1, source_target_pairs={{120,0},{0,8},{8,16},{16,24},{24,32},{32,40},{40,48},{48,56},{56,6... | collective-permute-start | bytes 1572872 | tf_op jit(solution)/shard_map/while/body/eval_jaxpr/ppermute | solution.py:19
  293.4 2.2 copy-start
  299.0 1.9 copy-start.1
  300.9 12.2 %collective-permute-start = (bf16[256,1024]{0,1:T(8,128)(2,1)S(1)}, bf16[256,1024]{0,1:T(8,128)(2,1)S(1)}, u32[]{:S(2)}, u32[]{:S(2)}) collective-permute-start(bf16[256,1024]{0,1:T(8,128)(2,1)S(1)} %get-tuple-element.538), channel_id=1, source_target_pairs={{120,0},{0,8},{8,16},{16,24},{24,32},{32,40},{40,48},{48,56},{56,6... | collective-permute-start | bytes 1572872 | tf_op jit(solution)/shard_map/while/body/eval_jaxpr/ppermute | solution.py:19
  314.7 2.2 copy-start
  320.3 1.9 copy-start.1
  322.2 12.2 %collective-permute-start = (bf16[256,1024]{0,1:T(8,128)(2,1)S(1)}, bf16[256,1024]{0,1:T(8,128)(2,1)S(1)}, u32[]{:S(2)}, u32[]{:S(2)}) collective-permute-start(bf16[256,1024]{0,1:T(8,128)(2,1)S(1)} %get-tuple-element.538), channel_id=1, source_target_pairs={{120,0},{0,8},{8,16},{16,24},{24,32},{32,40},{40,48},{48,56},{56,6... | collective-permute-start | bytes 1572872 | tf_op jit(solution)/shard_map/while/body/eval_jaxpr/ppermute | solution.py:19
  336.0 2.2 copy-start
  343.6 12.2 %collective-permute-start = (bf16[256,1024]{0,1:T(8,128)(2,1)S(1)}, bf16[256,1024]{0,1:T(8,128)(2,1)S(1)}, u32[]{:S(2)}, u32[]{:S(2)}) collective-permute-start(bf16[256,1024]{0,1:T(8,128)(2,1)S(1)} %get-tuple-element.538), channel_id=1, source_target_pairs={{120,0},{0,8},{8,16},{16,24},{24,32},{32,40},{40,48},{48,56},{56,6... | collective-permute-start | bytes 1572872 | tf_op jit(solution)/shard_map/while/body/eval_jaxpr/ppermute | solution.py:19
  357.3 2.2 copy-start
  364.9 12.2 %collective-permute-start = (bf16[256,1024]{0,1:T(8,128)(2,1)S(1)}, bf16[256,1024]{0,1:T(8,128)(2,1)S(1)}, u32[]{:S(2)}, u32[]{:S(2)}) collective-permute-start(bf16[256,1024]{0,1:T(8,128)(2,1)S(1)} %get-tuple-element.538), channel_id=1, source_target_pairs={{120,0},{0,8},{8,16},{16,24},{24,32},{32,40},{40,48},{48,56},{56,6... | collective-permute-start | bytes 1572872 | tf_op jit(solution)/shard_map/while/body/eval_jaxpr/ppermute | solution.py:19
  378.7 2.2 copy-start
  384.3 1.9 copy-start.1
  386.2 12.2 %collective-permute-start = (bf16[256,1024]{0,1:T(8,128)(2,1)S(1)}, bf16[256,1024]{0,1:T(8,128)(2,1)S(1)}, u32[]{:S(2)}, u32[]{:S(2)}) collective-permute-start(bf16[256,1024]{0,1:T(8,128)(2,1)S(1)} %get-tuple-element.538), channel_id=1, source_target_pairs={{120,0},{0,8},{8,16},{16,24},{24,32},{32,40},{40,48},{48,56},{56,6... | collective-permute-start | bytes 1572872 | tf_op jit(solution)/shard_map/while/body/eval_jaxpr/ppermute | solution.py:19
  400.0 2.2 copy-start
  407.5 12.2 %collective-permute-start = (bf16[256,1024]{0,1:T(8,128)(2,1)S(1)}, bf16[256,1024]{0,1:T(8,128)(2,1)S(1)}, u32[]{:S(2)}, u32[]{:S(2)}) collective-permute-start(bf16[256,1024]{0,1:T(8,128)(2,1)S(1)} %get-tuple-element.538), channel_id=1, source_target_pairs={{120,0},{0,8},{8,16},{16,24},{24,32},{32,40},{40,48},{48,56},{56,6... | collective-permute-start | bytes 1572872 | tf_op jit(solution)/shard_map/while/body/eval_jaxpr/ppermute | solution.py:19
  421.3 2.2 copy-start
  428.9 12.2 %collective-permute-start = (bf16[256,1024]{0,1:T(8,128)(2,1)S(1)}, bf16[256,1024]{0,1:T(8,128)(2,1)S(1)}, u32[]{:S(2)}, u32[]{:S(2)}) collective-permute-start(bf16[256,1024]{0,1:T(8,128)(2,1)S(1)} %get-tuple-element.538), channel_id=1, source_target_pairs={{120,0},{0,8},{8,16},{16,24},{24,32},{32,40},{40,48},{48,56},{56,6... | collective-permute-start | bytes 1572872 | tf_op jit(solution)/shard_map/while/body/eval_jaxpr/ppermute | solution.py:19
  442.6 2.2 copy-start
  448.3 1.9 copy-start.1
  450.2 12.2 %collective-permute-start = (bf16[256,1024]{0,1:T(8,128)(2,1)S(1)}, bf16[256,1024]{0,1:T(8,128)(2,1)S(1)}, u32[]{:S(2)}, u32[]{:S(2)}) collective-permute-start(bf16[256,1024]{0,1:T(8,128)(2,1)S(1)} %get-tuple-element.538), channel_id=1, source_target_pairs={{120,0},{0,8},{8,16},{16,24},{24,32},{32,40},{40,48},{48,56},{56,6... | collective-permute-start | bytes 1572872 | tf_op jit(solution)/shard_map/while/body/eval_jaxpr/ppermute | solution.py:19
  463.9 2.2 copy-start
  469.6 1.9 copy-start.1
  488.5 15.9 %copy-start.5 = (s32[256]{0:T(256)S(1)}, s32[256]{0:T(256)}, u32[]{:S(2)}) copy-start(s32[256]{0:T(256)} %copy-done.4) | copy-start | bytes 3076
  488.5 70.1 %all-to-all-start.3 = ((bf16[128,4,4096]{2,1,0:T(4,128)(2,1)}), bf16[128,4,4096]{2,1,0:T(4,128)(2,1)}, u32[]{:S(2)}, u32[]{:S(2)}) async-start(bf16[128,4,4096]{2,1,0:T(4,128)(2,1)} %reshape.374), calls=%async_computation.3 | async-start | bytes 8388608 | tf_op jit(solution)/shard_map/all_to_all | solution.py:199
  (6 other events, 9.8 us)
where the time goes:
time: 577 us; the launch traced here: 574 us
  waiting for transfers between devices  267 us (46%)
  local copies, waits for them, and re-layouts  113 us (20%)
  matrix products  79.2 us (14%)
  other arithmetic  60.5 us (10%)
  starting transfers between devices  51.8 us (9%)
    ppermute x15, waiting for transfers between devices, shifted(): return lax.ppermute(block, axis, route)  154 us
    dot_general x16, matrix products, absorb(): jnp.einsum('qhgk,khd->qhgd', weights.astype(jnp.bfloat16), value_portion,...  55.8 us
    all_to_all x1, waiting for transfers between devices, local(): lax.all_to_all(outgoing.reshape(devices, capacity, q_width), ('blk', 'gro...  54.2 us
    all_to_all x1, waiting for transfers between devices, local(): lax.all_to_all(send_q.reshape(devices, capacity, q_width), ('blk', 'group...  47.2 us
    while x90, local copies, waits for them, and re-layouts  33.9 us
    reduce_sum x16, other arithmetic, absorb(): row_total = row_total * decay_factor + jnp.sum(weights, -1)  28.6 us
    dot_general x16, matrix products, absorb(): jnp.einsum('qhgd,khd->qhgk', query_rotated, key_portion, preferred_elemen...  23.3 us
    all_to_all x1, starting transfers between devices, local(): lax.all_to_all(outgoing.reshape(devices, capacity, q_width), ('blk', 'gro...  15.9 us
  transfers between devices with their start and end apart: 19, of which 19 were waited for; matrix products, arithmetic and copies ran while one was open for 5% of the time, Pallas kernels for 0%

commit v1 on v0

v1 whole, which is shorter than its diff:
```python
import math

import jax
import jax.numpy as jnp
from jax import lax
from jax.experimental import pallas as pl
from jax.experimental.pallas import tpu as pltpu
from jax.sharding import PartitionSpec as P

QUERY_HEADS = 32
KEY_VALUE_HEADS = 4
HEAD_SIZE = 128
THETA = 500000.0

TOK = 256
SLOT = 64
KEYS = 512
BLOCK = 256
TILE = 32
SUPER = 256
HALF = QUERY_HEADS // 2 * HEAD_SIZE
WIDE = HALF + 128
ROWS = 16 * SLOT
NEG = -1e30
SCALE = math.log2(math.e) / math.sqrt(HEAD_SIZE)
MESH = pl.DeviceIdType.MESH
VMEM_LIMIT = 60 * 1024 * 1024


def coords():
    b = lax.axis_index("blk")
    g = lax.axis_index("group")
    return b // 4, g % 4, (b // 2) % 2 * 2 + g // 4, b % 2


def device(x, y, z, core):
    x, y, z = lax.rem(x + 4, 4), lax.rem(y + 4, 4), lax.rem(z + 4, 4)
    return x * 4 + z // 2 * 2 + core, lax.rem(z, 2) * 4 + y


def moved(sign, delta, core):
    x, y, z, _ = coords()
    return device(x + sign * (delta // 4), y + sign * (delta // 2 % 2), z + sign * (delta % 2), core)


def opposite(bit):
    x, y, z, core = coords()
    return device(x + 2 * (bit == 4), y + 2 * (bit == 2), z + 2 * (bit == 1), core)


def sign_of(core):
    return 1 - 2 * core


def signal(target):
    pl.semaphore_signal(pltpu.get_barrier_semaphore(), inc=1, device_id=target, device_id_type=MESH)


def remote(src, dst, send, recv, target):
    return pltpu.make_async_remote_copy(
        src_ref=src, dst_ref=dst, send_sem=send, recv_sem=recv, device_id=target, device_id_type=MESH
    )


THIRDS = ((0, 176, (4, 2, 1)), (176, 176, (2, 1, 4)), (352, 160, (1, 4, 2)))


def exchange_kernel(q_ref, kv_ref, got_ref, all_ref, q_send, q_recv, kv_send, kv_recv, local_sem):
    x, y, z, core = coords()
    place = x // 2 * 4 + y // 2 * 2 + z // 2
    mine = sign_of(core)
    other = 1 - core

    for delta in range(1, 8):
        for source in range(2):
            signal(moved(-sign_of(source), delta, source))
    signal(moved(0, 0, other))
    for bit in (4, 2, 1):
        signal(opposite(bit))
    pl.semaphore_wait(pltpu.get_barrier_semaphore(), 18)

    own_q = pltpu.make_async_copy(
        q_ref.at[0, :, pl.ds(pl.multiple_of(core * WIDE, 128), WIDE)], got_ref.at[0, core], local_sem.at[0]
    )
    own_kv = pltpu.make_async_copy(kv_ref, all_ref.at[place], local_sem.at[1])
    own_kv.start()
    own_q.start()

    def flip(mask):
        out = 0
        for bit in (4, 2, 1):
            digit = place // bit % 2
            out = out + bit * ((1 - digit) if mask & bit else digit)
        return out

    def kv_copy(third, index):
        start, size, (b1, b2, b3) = THIRDS[third]
        mask, axis = ((0, b1), (0, b2), (0, b3), (b1, b2), (b1, b3), (b2, b3), (b1 ^ b2, b3))[index]
        rows = pl.ds(start, size)
        block = flip(mask)
        src = kv_ref.at[rows] if mask == 0 else all_ref.at[block, rows]
        return remote(
            src, all_ref.at[block, rows], kv_send.at[third, index], kv_recv.at[third, index], opposite(axis)
        )

    def kv_landed(third, index):
        start, size, (b1, b2, b3) = THIRDS[third]
        mask = (b1, b2, b3, b1 ^ b2, b1 ^ b3, b2 ^ b3, 7)[index]
        here = all_ref.at[flip(mask), pl.ds(start, size)]
        remote(here, here, kv_send.at[third, index], kv_recv.at[third, index], opposite(4)).wait_recv()

    copies = []

    def start(copy):
        copy.start()
        copies.append(copy)

    for index in range(3):
        for third in range(3):
            start(kv_copy(third, index))

    def q_copy(delta, to_core, target):
        columns = pl.ds(pl.multiple_of(to_core * WIDE, 128), WIDE)
        slot = delta * 2 + to_core if delta else 0
        return remote(
            q_ref.at[delta, :, columns], got_ref.at[delta, core], q_send.at[slot], q_recv.at[delta, core], target
        )

    start(q_copy(0, other, moved(0, 0, other)))
    for delta in (7, 6, 5, 3, 4, 2, 1):
        for to_core in range(2):
            start(q_copy(delta, to_core, moved(mine, delta, to_core)))

    for third in range(3):
        kv_landed(third, 0)
        start(kv_copy(third, 3))
        start(kv_copy(third, 4))
    for third in range(3):
        kv_landed(third, 1)
        start(kv_copy(third, 5))
    for third in range(3):
        kv_landed(third, 3)
        start(kv_copy(third, 6))
    for index in (2, 4, 5, 6):
        for third in range(3):
            kv_landed(third, index)

    def q_landed(delta, source):
        here = got_ref.at[delta, source]
        remote(here, here, q_send.at[0], q_recv.at[delta, source], moved(0, 0, other)).wait_recv()

    q_landed(0, other)
    for delta in range(1, 8):
        for source in range(2):
            q_landed(delta, source)
    own_q.wait()
    own_kv.wait()
    for copy in copies:
        copy.wait_send()


def exchange(q, kv):
    return pl.pallas_call(
        exchange_kernel,
        out_shape=(
            jax.ShapeDtypeStruct((8, 2, SLOT, WIDE), jnp.bfloat16),
            jax.ShapeDtypeStruct((8, KEYS, 512), jnp.bfloat16),
        ),
        in_specs=[pl.BlockSpec(memory_space=pl.ANY)] * 2,
        out_specs=[pl.BlockSpec(memory_space=pl.ANY)] * 2,
        scratch_shapes=[
            pltpu.SemaphoreType.DMA((16,)),
            pltpu.SemaphoreType.DMA((8, 2)),
            pltpu.SemaphoreType.DMA((3, 7)),
            pltpu.SemaphoreType.DMA((3, 7)),
            pltpu.SemaphoreType.DMA((2,)),
        ],
        compiler_params=pltpu.CompilerParams(collective_id=0, has_side_effects=True),
        name="exchange",
    )(q, kv)


def back_kernel(out_ref, ret_ref, send, recv, local_sem):
    x, y, z, core = coords()
    mine = sign_of(core)
    other = 1 - core
    for delta in range(1, 8):
        for worker in range(2):
            signal(moved(mine, delta, worker))
    signal(moved(0, 0, other))
    pl.semaphore_wait(pltpu.get_barrier_semaphore(), 15)

    columns = pl.ds(pl.multiple_of(core * HALF, 128), HALF)
    own = pltpu.make_async_copy(out_ref.at[0, core], ret_ref.at[0, :, columns], local_sem)
    own.start()
    copies = [
        remote(
            out_ref.at[0, other],
            ret_ref.at[0, :, columns],
            send.at[0],
            recv.at[0, core],
            moved(0, 0, other),
        )
    ]
    for delta in (7, 6, 5, 3, 4, 2, 1):
        for source in range(2):
            copies.append(
                remote(
                    out_ref.at[delta, source],
                    ret_ref.at[delta, :, columns],
                    send.at[delta * 2 + source],
                    recv.at[delta, core],
                    moved(-sign_of(source), delta, source),
                )
            )
    for copy in copies:
        copy.start()

    def landed(delta, worker):
        here = ret_ref.at[delta, :, pl.ds(pl.multiple_of(worker * HALF, 128), HALF)]
        remote(here, here, send.at[0], recv.at[delta, worker], moved(0, 0, other)).wait_recv()

    landed(0, other)
    for delta in range(1, 8):
        for worker in range(2):
            landed(delta, worker)
    own.wait()
    for copy in copies:
        copy.wait_send()


def back(out):
    return pl.pallas_call(
        back_kernel,
        out_shape=jax.ShapeDtypeStruct((8, SLOT, 2 * HALF), jnp.bfloat16),
        in_specs=[pl.BlockSpec(memory_space=pl.ANY)],
        out_specs=pl.BlockSpec(memory_space=pl.ANY),
        scratch_shapes=[
            pltpu.SemaphoreType.DMA((16,)),
            pltpu.SemaphoreType.DMA((8, 2)),
            pltpu.SemaphoreType.DMA(()),
        ],
        compiler_params=pltpu.CompilerParams(collective_id=1, has_side_effects=True),
        name="back",
    )(out)


def attend_kernel(
    low_ref, high_ref, count_ref, rank_row, rank_col, u_ref, begin_ref, cos_ref, sin_ref, q_ref, kv_ref,
    out_ref, turned, made, peak, total,
):
    ones = jnp.ones((BLOCK, HEAD_SIZE), jnp.bfloat16)
    out_ref[...] = jnp.zeros_like(out_ref)
    lanes = lax.broadcasted_iota(jnp.int32, (TILE * 8, BLOCK), 1)

    def one_super(sup, carry):
        base = pl.multiple_of(sup * SUPER, SUPER)
        pick = (
            lax.broadcasted_iota(jnp.int32, (SUPER, ROWS), 0) + base == rank_row[...]
        ).astype(jnp.bfloat16)
        cos = cos_ref[pl.ds(base, SUPER), :]
        sin = sin_ref[pl.ds(base, SUPER), :]
        for head in range(2):
            for part in range(2):
                columns = slice(head * 1024 + part * 512, head * 1024 + part * 512 + 512)
                rows = jnp.dot(pick, q_ref[:, columns], preferred_element_type=jnp.float32)
                for one in range(4):
                    entry = rows[:, one * HEAD_SIZE : (one + 1) * HEAD_SIZE]
                    entry = entry * cos + pltpu.roll(entry, HEAD_SIZE // 2, 1) * sin
                    turned[head, part * 4 + one] = entry.astype(jnp.bfloat16)

        def one_tile(tile, carry):
            first = pl.multiple_of(tile * TILE, TILE)
            where = pl.multiple_of(base + first, TILE)
            low = low_ref[sup * (SUPER // TILE) + tile]
            high = high_ref[sup * (SUPER // TILE) + tile]
            begin = begin_ref[pl.ds(where, TILE), :]
            begin = jnp.concatenate([begin] * 8, 0)
            last = u_ref[pl.ds(where, TILE), :]
            last = jnp.concatenate([last] * 8, 0)
            peak[...] = jnp.full_like(peak, NEG)
            total[...] = jnp.zeros_like(total)

            def one_block(block, carry):
                holder = jnp.where(block < 8, block, 15 - block)
                rows = pl.ds(pl.multiple_of(jnp.where(block < 8, 0, BLOCK), BLOCK), BLOCK)
                place = lanes + block * BLOCK
                allowed = (place >= begin) & (place <= last)
                for head in range(2):
                    query = turned[head, :, pl.ds(first, TILE), :].reshape(TILE * 8, HEAD_SIZE)
                    key = kv_ref[holder, rows, head * HEAD_SIZE : (head + 1) * HEAD_SIZE]
                    value = kv_ref[holder, rows, (2 + head) * HEAD_SIZE : (3 + head) * HEAD_SIZE]
                    score = lax.dot_general(
                        query, key, (((1,), (1,)), ((), ())), preferred_element_type=jnp.float32
                    )
                    score = jnp.where(allowed, score, NEG)
                    old = peak[head]
                    new = jnp.maximum(old, jnp.max(score, 1, keepdims=True))
                    weight = jnp.exp2(score - jnp.concatenate([new, new], 1)).astype(jnp.bfloat16)
                    decay = jnp.exp2(old - new)
                    peak[head] = new
                    total[head] = total[head] * jnp.concatenate([decay, decay], 1) + jnp.dot(
                        weight, jnp.concatenate([value, ones], 1), preferred_element_type=jnp.float32
                    )
                return carry

            lax.fori_loop(low, high + 1, one_block, 0)
            for head in range(2):
                result = total[head, :, :HEAD_SIZE] / jnp.maximum(total[head, :, HEAD_SIZE:], 1e-30)
                result = result.astype(jnp.bfloat16)
                for one in range(8):
                    made[pl.ds(first, TILE), pl.ds((head * 8 + one) * HEAD_SIZE, HEAD_SIZE)] = result[
                        one * TILE : (one + 1) * TILE
                    ]
            return carry

        lax.fori_loop(0, SUPER // TILE, one_tile, 0)
        put = (
            lax.broadcasted_iota(jnp.int32, (ROWS, SUPER), 1) + base == rank_col[...]
        ).astype(jnp.bfloat16)
        for part in range(4):
            columns = slice(part * 512, part * 512 + 512)
            out_ref[:, columns] += jnp.dot(put, made[:, columns], preferred_element_type=jnp.float32).astype(
                jnp.bfloat16
            )
        return carry

    lax.fori_loop(0, count_ref[0], one_super, 0)


def attend(low, high, count, rank, u, begin, cos, sin, q, kv):
    smem = pl.BlockSpec(memory_space=pltpu.SMEM)
    vmem = pl.BlockSpec(memory_space=pltpu.VMEM)
    return pl.pallas_call(
        attend_kernel,
        out_shape=jax.ShapeDtypeStruct((ROWS, HALF), jnp.bfloat16),
        in_specs=[smem] * 3 + [vmem] * 8,
        out_specs=vmem,
        scratch_shapes=[
            pltpu.VMEM((2, 8, SUPER, HEAD_SIZE), jnp.bfloat16),
            pltpu.VMEM((SUPER, HALF), jnp.bfloat16),
            pltpu.VMEM((2, TILE * 8, HEAD_SIZE), jnp.float32),
            pltpu.VMEM((2, TILE * 8, 2 * HEAD_SIZE), jnp.float32),
        ],
        compiler_params=pltpu.CompilerParams(vmem_limit_bytes=VMEM_LIMIT),
        name="attend",
    )(low, high, count, rank[None, :], rank[:, None], u[:, None], begin[:, None], cos, sin, q, kv)


def document_start(u, lengths):
    ends = jnp.cumsum(lengths)
    return jnp.sum(jnp.where(u[:, None] >= ends[None, :], lengths[None, :], 0), 1)


def angles_of(position):
    half = HEAD_SIZE // 2
    inv_freq = jnp.exp(-jnp.log(THETA) * (2.0 * jnp.arange(half, dtype=jnp.float32) / HEAD_SIZE))
    angle = position.astype(jnp.float32)[:, None] * inv_freq[None, :]
    return jnp.cos(angle), jnp.sin(angle)


def one_hot(index, size):
    return (jnp.arange(size, dtype=jnp.int32)[:, None] == index[None, :]).astype(jnp.bfloat16)


def local(queries, keys, values, plan, doc_lengths):
    x, y, z, core = coords()
    my_cycle = x % 2 * 4 + y % 2 * 2 + z % 2
    my_place = x // 2 * 4 + y // 2 * 2 + z // 2

    owner = plan // TOK
    cycle = owner % 8
    p = owner // 8
    offset = plan % TOK
    front = offset < 128
    u = jnp.where(front, p * 128 + offset, (31 - p) * 128 + offset - 128)
    place = p // 2
    row = jnp.where(front, p % 2 * 128 + offset, 256 + (1 - p % 2) * 128 + offset - 128)
    order = jnp.arange(TOK, dtype=jnp.int32)
    earlier = order[None, :] < order[:, None]
    rank_slot = jnp.sum((earlier & (owner[:, None] == owner[None, :])).astype(jnp.int32), 1)
    rank_cycle = jnp.sum((earlier & (cycle[:, None] == cycle[None, :])).astype(jnp.int32), 1)
    to_x = place // 4 * 2 + cycle // 4
    to_y = place // 2 % 2 * 2 + cycle // 2 % 2
    to_z = place % 2 * 2 + cycle % 2
    chip = (to_x * 2 + to_z // 2) * 8 + to_z % 2 * 4 + to_y
    send_kv = one_hot(chip * 8 + p % 2 * 4 + rank_slot, 512)
    delta = jnp.bitwise_xor(cycle, my_cycle)
    send_q = one_hot(delta * SLOT + rank_cycle, 8 * SLOT)

    fields = jnp.stack([jnp.where(row < 256, row + 1, 0), jnp.where(row < 256, 0, row - 255)], 1)
    fields = jnp.pad(fields, ((0, 0), (0, 126))).astype(jnp.bfloat16)
    lengths = doc_lengths[0]
    known = jnp.concatenate([lengths // 256, lengths % 256])
    known = jnp.pad(known, (512 + 2, 128 - 2 - 8)).astype(jnp.bfloat16)
    halves = []
    for half in range(2):
        columns = slice(half * 256, half * 256 + 256)
        table = jnp.concatenate([keys[:, columns], values[:, columns], fields], 1)
        sent = jnp.dot(send_kv, table, preferred_element_type=jnp.float32).astype(jnp.bfloat16)
        halves.append((sent + known[None, :]).reshape(8, 1, 8, 8, 640))
    got = lax.all_to_all(
        jnp.concatenate(halves, 1).reshape(128, 8, 640),
        ("blk", "group"),
        split_axis=0,
        concat_axis=0,
        tiled=True,
    )
    known = lax.dynamic_slice(got, (my_cycle, 0, 512 + 2), (1, 1, 8)).reshape(8).astype(jnp.int32)
    lengths = known[:4] * 256 + known[4:]
    got = got.reshape(1024, 640)
    lower = got[:, 512].astype(jnp.int32)
    upper = got[:, 513].astype(jnp.int32)
    row = jnp.where(lower > 0, lower - 1, jnp.where(upper > 0, upper + 255, -1))
    kv = jnp.dot(one_hot(row, KEYS), got[:, :512], preferred_element_type=jnp.float32)
    rows = jnp.arange(KEYS, dtype=jnp.int32)
    key_u = jnp.where(rows < 256, my_place * 256 + rows, (15 - my_place) * 256 + rows - 256)
    cosine, sine = angles_of(key_u - document_start(key_u, lengths))
    cosine, sine = cosine[:, None, :], sine[:, None, :]
    k = kv[:, :256].reshape(KEYS, 2, HEAD_SIZE)
    a, b = k[..., :64], k[..., 64:]
    k = jnp.concatenate([a * cosine - b * sine, b * cosine + a * sine], -1)
    kv = jnp.concatenate([k.reshape(KEYS, 256), kv[:, 256:]], 1).astype(jnp.bfloat16)

    fields = jnp.pad(jnp.stack([u // 256 + 1, u % 256], 1), ((0, 0), (0, 126))).astype(jnp.bfloat16)
    table = jnp.concatenate([queries[:, :HALF], fields, queries[:, HALF:], fields], 1)
    q = jnp.dot(send_q, table, preferred_element_type=jnp.float32).astype(jnp.bfloat16)
    q, kv = exchange(q.reshape(8, SLOT, 2 * WIDE), kv)
    q = q.reshape(ROWS, WIDE)

    lead = q[:, HALF].astype(jnp.int32)
    u = (lead - 1) * 256 + q[:, HALF + 1].astype(jnp.int32)
    valid = lead > 0
    index = jnp.arange(ROWS, dtype=jnp.int32)
    sort_key = jnp.where(valid, u, 4096 + index)
    rank = jnp.sum((sort_key[None, :] < sort_key[:, None]).astype(jnp.int32), 1)
    sorted_u = jnp.sum(jnp.where(index[:, None] == rank[None, :], sort_key[None, :], 0), 1)
    count = jnp.sum(valid.astype(jnp.int32))
    live = sorted_u < 4096
    begin = jnp.where(live, document_start(sorted_u, lengths), 8192)
    cosine, sine = angles_of(jnp.where(live, sorted_u - begin, 0))
    cosine = jnp.concatenate([cosine, cosine], 1) * SCALE
    sine = jnp.concatenate([-sine, sine], 1) * SCALE
    low = jnp.where(live, begin // BLOCK, 0).reshape(ROWS // TILE, TILE)[:, 0]
    high = jnp.max(jnp.where(live, sorted_u // BLOCK, -1).reshape(ROWS // TILE, TILE), 1)
    supers = (count + SUPER - 1) // SUPER
    out = attend(low, high, supers.reshape(1), rank, sorted_u, begin, cosine, sine, q, kv)

    ret = back(out.reshape(8, 2, SLOT, HALF)).reshape(8 * SLOT, 2 * HALF)
    return lax.dot_general(
        send_q, ret, (((0,), (0,)), ((), ())), preferred_element_type=jnp.float32
    ).astype(jnp.bfloat16)


def solution(mesh):
    return jax.shard_map(
        local,
        mesh=mesh,
        in_specs=(
            P(("blk", "group"), None),
            P(("blk", "group"), None),
            P(("blk", "group"), None),
            P(("blk", "group")),
            P("group", None),
        ),
        out_specs=P(("blk", "group"), None),
        check_vma=False,
    )
```

time: 577 us -> 214 us (0.37)
  waiting for transfers between devices: 267 us -> 17.6 us
  Pallas kernels: 0 us -> 150 us
  local copies, waits for them, and re-layouts: 113 us -> 5.25 us
  matrix products: 79.2 us -> 10.3 us
  other arithmetic: 60.5 us -> 18 us
  starting transfers between devices: 51.8 us -> 11.5 us
    ppermute x15 -> x0, waiting for transfers between devices: 154 us -> none  [shifted(): return lax.ppermute(block, axis, route)]
    pallas_call x0 -> x3, Pallas kernels: none -> 150 us  [the longest x1 50.5 us: exchange(): pl.pallas_call(exchange_kernel, out_shape=(jax.ShapeDtypeStruct((8, 2, SL...]
    all_to_all x4 -> x1, waiting for transfers between devices: 113 us -> 17.6 us  [local(): lax.all_to_all(jnp.concatenate(halves, 1).reshape(128, 8, 640), ('blk', '...]
    dot_general x32 -> x5, matrix products: 79.2 us -> 10.3 us  [the longest x1 4.81 us: local(): lax.dot_general(send_q, ret, (((0,), (0,)), ((), ())), preferred_element_...]
    while x90 -> x0, local copies, waits for them, and re-layouts: 33.9 us -> none
    reshape x7 -> x0, local copies, waits for them, and re-layouts: 30.1 us -> none  [the longest x1 7.19 us: local(): send_q.reshape(devices, capacity, q_width)]
    gather x7 -> x0, local copies, waits for them, and re-layouts: 30 us -> none  [the longest x1 7.93 us: local(): return returned[buffer_index]]
    reduce_sum x34 -> x7, other arithmetic: 30.3 us -> 2.22 us  [the longest x1 0.63 us: local(): count = jnp.sum(valid.astype(jnp.int32))]
  transfers between devices with their start and end apart: 19 -> 1, of which waited for: 19 -> 1; matrix products, arithmetic and copies ran while one was open for 5% -> 2% of each run, Pallas kernels for 0% -> 0%
where the time goes in v1:
time: 214 us
  Pallas kernels  150 us (70%)
  other arithmetic  18 us (8%)
  waiting for transfers between devices  17.6 us (8%)
  starting transfers between devices  11.5 us (5%)
  matrix products  10.3 us (5%)
  local copies, waits for them, and re-layouts  5.25 us (2%)
    pallas_call x1, Pallas kernels, exchange(): pl.pallas_call(exchange_kernel, out_shape=(jax.ShapeDtypeStruct((8, 2, SL...  50.5 us
    pallas_call x1, Pallas kernels, back(): pl.pallas_call(back_kernel, out_shape=jax.ShapeDtypeStruct((8, SLOT, 2 *...  50.3 us
    pallas_call x1, Pallas kernels, attend(): pl.pallas_call(attend_kernel, out_shape=jax.ShapeDtypeStruct((ROWS, HALF)...  49 us
    all_to_all x1, waiting for transfers between devices, local(): lax.all_to_all(jnp.concatenate(halves, 1).reshape(128, 8, 640), ('blk', '...  17.6 us
    all_to_all x1, starting transfers between devices, local(): lax.all_to_all(jnp.concatenate(halves, 1).reshape(128, 8, 640), ('blk', '...  11.5 us
    dot_general x1, matrix products, local(): lax.dot_general(send_q, ret, (((0,), (0,)), ((), ())), preferred_element_...  4.81 us
  transfers between devices with their start and end apart: 1, of which 1 were waited for; matrix products, arithmetic and copies ran while one was open for 2% of the time, Pallas kernels for 0%

profile of v1, /device:TPU:1, one launch (start us, length us, event | category | flops | bytes accessed | tf_op | source)
XLA Modules:
  0.0 213.5 jit_solution(2146068951093399068)
XLA Ops:
  0.0 0.7 and_select_fusion.19
  0.7 0.2 convert_reduce_fusion.1
  0.9 0.7 fusion.64
  1.5 0.7 add_add_fusion
  2.3 0.2 convert_reduce_fusion.2
  2.5 0.7 select_convert_fusion.2
  3.2 0.1 copy.49
  3.4 0.1 fusion.51
  3.5 1.1 fusion.74
  4.6 0.4 fusion.8
  5.0 0.4 fusion.9
  5.4 0.1 pad_maximum_fusion
  5.5 1.2 copy.38
  6.7 11.5 %all-to-all-start = ((bf16[128,8,640]{2,1,0:T(8,128)(2,1)}), bf16[128,8,640]{2,1,0:T(8,128)(2,1)S(1)}, u32[]{:S(2)}, u32[]{:S(2)}) async-start(bf16[128,8,640]{2,1,0:T(8,128)(2,1)} %bitcast.4), calls=%async_computation | async-start | bytes 2621440 | tf_op jit(solution)/shard_map/all_to_all | solution.py:402
  18.3 0.1 copy.48
  18.6 0.2 fusion.72
  18.8 3.9 %convolution_convert_fusion = bf16[512,4352]{1,0:T(8,128)(2,1)} fusion(bf16[256,128]{1,0:T(8,128)(2,1)S(1)} %pad.14.clone, bf16[256,2048]{1,0:T(8,128)(2,1)S(1)} %get-tuple-element.23, bf16[256,2048]{1,0:T(8,128)(2,1)S(1)} %get-tuple-element.22, s32[256]{0:T(256)S(1)} %get-tuple-element.45), kind=kOutput, calls=%fused_computation | convolution fusion | flops 1152122880 | bytes 6620160 | tf_op jit(solution)/shard_map/dot_general | solution.py:427
  22.7 17.6 %all-to-all-done = bf16[128,8,640]{2,1,0:T(8,128)(2,1)S(1)} async-done(((bf16[128,8,640]{2,1,0:T(8,128)(2,1)}), bf16[128,8,640]{2,1,0:T(8,128)(2,1)S(1)}, u32[]{:S(2)}, u32[]{:S(2)}) %all-to-all-start) | async-done | bytes 1310752 | tf_op jit(solution)/shard_map/all_to_all | solution.py:402
  40.6 0.4 fusion.14
  41.0 0.8 fusion.7
  41.9 0.2 reduce-window.8
  42.0 0.1 select_reduce_fusion.3
  42.1 0.1 copy.50
  42.3 0.2 copy.47
  42.6 0.2 copy.46
  42.8 1.0 multiply_cosine_fusion.1
  43.8 0.6 subtract_convert_fusion
  44.4 0.7 pad_maximum_fusion.2
  45.1 0.8 pad_maximum_fusion.1.kv_ref
  46.0 50.5 %exchange.1 = (bf16[8,2,64,2176]{3,2,1,0:T(8,128)(2,1)}, bf16[8,512,512]{2,1,0:T(8,128)(2,1)}) custom-call(bf16[8,64,4352]{2,1,0:T(8,128)(2,1)} %bitcast.46, bf16[512,512]{1,0:T(8,128)(2,1)} %pad_maximum_fusion.1.kv_ref), custom_call_target="tpu_custom_call" | custom-call | tf_op jit(solution)/shard_map/exchange/pallas_call | solution.py:163
  96.5 1.2 fusion.29
  97.6 1.6 select_reduce_fusion.1
  99.2 0.6 convert_reduce_fusion.3
  100.5 0.6 convert_reduce_fusion
  101.1 0.5 select_reduce_fusion
  101.6 0.1 select_reduce_fusion.2
  101.8 0.6 fusion.44
  102.5 0.2 copy.45.u_ref
  102.7 0.2 copy.43
  102.9 1.0 copy.44.rank_col
  104.0 1.9 fusion.36
  105.9 1.0 maximum_multiply_fusion.cos_ref
  106.9 0.9 compare_select_fusion.begin_ref
  107.8 1.0 maximum_multiply_fusion.1.sin_ref
  108.8 0.7 fusion.41.low_ref
  109.4 49.0 %attend.1 = bf16[1024,2048]{1,0:T(8,128)(2,1)} custom-call(s32[32]{0:T(128)} %fusion.41.low_ref, s32[32]{0:T(128)} %get-tuple-element.11.high_ref, s32[1]{0:T(128)} %bitcast.11.count_ref, s32[1,1024]{1,0:T(1,128)} %bitcast.57, s32[1024,1]{1,0:T(8,128)} %copy.44.rank_col, s32[1024,1]{1,0:T(8,128)} %copy-done, s32[1024,1]{1,0:T(8,128)} %compare_select_fusion.begin_ref, ...), custom_call_target="tpu_custom_call" | custom-call | tf_op jit(solution)/shard_map/attend/pallas_call | solution.py:334
  158.4 50.3 %back.1 = bf16[8,64,4096]{2,1,0:T(8,128)(2,1)} custom-call(bf16[8,2,64,2048]{3,2,1,0:T(8,128)(2,1)} %bitcast.42), custom_call_target="tpu_custom_call" | custom-call | tf_op jit(solution)/shard_map/back/pallas_call | solution.py:233
  208.7 4.8 %convolution_convert_fusion.1 = bf16[256,4096]{1,0:T(8,128)(2,1)} fusion(bf16[512,4096]{1,0:T(8,128)(2,1)} %bitcast.41, s32[256]{0:T(256)S(1)} %get-tuple-element.45), kind=kOutput, calls=%fused_computation.1 | convolution fusion | flops 1074921472 | bytes 6292480 | tf_op jit(solution)/shard_map/dot_general | solution.py:450
  (30 shorter events, 0.6 us)
Async XLA Ops:
  5.4 13.2 %copy-start.1 = (bf16[256,4096]{1,0:T(8,128)(2,1)S(1)}, bf16[256,4096]{1,0:T(8,128)(2,1)}, u32[]{:S(2)}) copy-start(bf16[256,4096]{1,0:T(8,128)(2,1)} %param.5) | copy-start | bytes 6291460
  6.7 33.7 %all-to-all-start = ((bf16[128,8,640]{2,1,0:T(8,128)(2,1)}), bf16[128,8,640]{2,1,0:T(8,128)(2,1)S(1)}, u32[]{:S(2)}, u32[]{:S(2)}) async-start(bf16[128,8,640]{2,1,0:T(8,128)(2,1)} %bitcast.4), calls=%async_computation | async-start | bytes 2621440 | tf_op jit(solution)/shard_map/all_to_all | solution.py:402
  101.1 8.4 %copy-start.2 = (s32[1024]{0:T(1024)}, s32[1024]{0:T(1024)S(1)}, u32[]{:S(2)}) copy-start(s32[1024]{0:T(1024)S(1)} %convert_reduce_fusion) | copy-start | bytes 12292
  102.7 6.7 %copy-start = (s32[1024,1]{1,0:T(8,128)}, s32[1024,1]{1,0:T(8,128)S(1)}, u32[]{:S(2)}) copy-start(s32[1024,1]{1,0:T(8,128)S(1)} %copy.45.u_ref) | copy-start | bytes 12292

commit v2 on v1

v2 whole, which is shorter than its diff:
```python
import math

import jax
import jax.numpy as jnp
from jax import lax
from jax.experimental import pallas as pl
from jax.experimental.pallas import tpu as pltpu
from jax.sharding import PartitionSpec as P

QUERY_HEADS = 32
KEY_VALUE_HEADS = 4
HEAD_SIZE = 128
THETA = 500000.0

TOK = 256
SLOT = 64
KEYS = 512
BLOCK = 256
TILE = 32
SUPER = 256
HALF = QUERY_HEADS // 2 * HEAD_SIZE
WIDE = HALF + 128
ROWS = 16 * SLOT
NEG = -1e30
SCALE = math.log2(math.e) / math.sqrt(HEAD_SIZE)
MESH = pl.DeviceIdType.MESH
VMEM_LIMIT = 60 * 1024 * 1024


def coords():
    b = lax.axis_index("blk")
    g = lax.axis_index("group")
    return b // 4, g % 4, (b // 2) % 2 * 2 + g // 4, b % 2


def device(x, y, z, core):
    x, y, z = lax.rem(x + 4, 4), lax.rem(y + 4, 4), lax.rem(z + 4, 4)
    return x * 4 + z // 2 * 2 + core, lax.rem(z, 2) * 4 + y


def moved(sign, delta, core):
    x, y, z, _ = coords()
    return device(x + sign * (delta // 4), y + sign * (delta // 2 % 2), z + sign * (delta % 2), core)


def sign_of(core):
    return 1 - 2 * core


def signal(target):
    pl.semaphore_signal(pltpu.get_barrier_semaphore(), inc=1, device_id=target, device_id_type=MESH)


def remote(src, dst, send, recv, target):
    return pltpu.make_async_remote_copy(
        src_ref=src, dst_ref=dst, send_sem=send, recv_sem=recv, device_id=target, device_id_type=MESH
    )


THIRDS = ((0, 176, (4, 2, 1)), (176, 176, (2, 1, 4)), (352, 160, (1, 4, 2)))
PAIR = 640
PART = 128


def iota(shape, axis):
    return lax.broadcasted_iota(jnp.int32, shape, axis)


def bf16(flags):
    return jnp.where(flags, 1.0, 0.0).astype(jnp.bfloat16)


def dot(a, b):
    return jnp.dot(a, b, preferred_element_type=jnp.float32)


def cycle_of(plan):
    return (plan >> 8) & 7


def cycle_index(plan):
    p = plan >> 11
    offset = plan & 255
    return jnp.where(offset < 128, p * 128 + offset, (31 - p) * 128 + offset - 128)


def document_start(u, lengths):
    end = jnp.zeros((1, 1), jnp.int32)
    start = jnp.zeros_like(u)
    for one in range(4):
        length = lengths[0:1, one : one + 1]
        end = end + length
        start = start + jnp.where(u >= end, length, 0)
    return start


def turning(position):
    half = HEAD_SIZE // 2
    lane = iota((1, HEAD_SIZE), 1)
    spot = (lane & (half - 1)).astype(jnp.float32)
    inv_freq = jnp.exp(-math.log(THETA) * (2.0 * spot / HEAD_SIZE))
    angle = position.astype(jnp.float32) * inv_freq
    both = jnp.cos(jnp.where(lane < half, angle, angle - math.pi / 2))
    other = pltpu.roll(both, half, 1)
    first = jnp.broadcast_to(lane < half, both.shape)
    return jnp.where(first, both, other), jnp.where(first, -other, both)


def exchange_kernel(
    queries_ref, keys_ref, values_ref, plan_col, plan_row, lengths_ref,
    sorted_ref, all_ref, places_ref, rank_ref,
    q_out, q_got, kv_out, kv_got, part_out, part_got, own_ref, len_got, key_ref, cos_ref, sin_ref,
    q_send, q_recv, a_send, a_recv, b_send, b_recv, kv_send, kv_recv, len_send, len_recv, local_sem,
):
    x, y, z, core = coords()
    place = x // 2 * 4 + y // 2 * 2 + z // 2
    my_cycle = x % 2 * 4 + y % 2 * 2 + z % 2
    mine = sign_of(core)
    other = 1 - core

    block_at, group_at = lax.axis_index("blk"), lax.axis_index("group")
    spot = block_at // 2
    to_device = device(
        spot // 4 * 2 + group_at // 4, spot // 2 % 2 * 2 + group_at // 2 % 2, spot % 2 * 2 + group_at % 2, block_at % 2
    )
    from_block = place * 2 + core
    at_home = (from_block == block_at) & (my_cycle == group_at)

    for delta in range(1, 8):
        for source in range(2):
            signal(moved(-sign_of(source), delta, source))
    signal(moved(0, 0, other))
    for mask in range(1, 8):
        signal(across_cycle(mask))

    @pl.when(jnp.logical_not(at_home))
    def _():
        signal((from_block, my_cycle))

    plan_c, plan_r = plan_col[...], plan_row[...]
    same = (cycle_of(plan_c) == cycle_of(plan_r)) & (iota((TOK, TOK), 0) < iota((TOK, TOK), 1))
    rank = jnp.sum(jnp.where(same, 1, 0), 0, keepdims=True)
    row = jnp.bitwise_xor(cycle_of(plan_r), my_cycle) * SLOT + rank
    choose = bf16(iota((8 * SLOT, TOK), 0) == row)
    u = cycle_index(plan_c)
    lane = iota((TOK, 128), 1)
    fields = jnp.where(lane == 0, (u >> 8) + 1, jnp.where(lane == 1, u & 255, 0))
    fields = fields.astype(jnp.float32).astype(jnp.bfloat16)
    chosen_k = dot(choose, keys_ref[...]).astype(jnp.bfloat16)
    chosen_v = dot(choose, values_ref[...]).astype(jnp.bfloat16)
    chosen_f = dot(choose, fields).astype(jnp.bfloat16)
    for delta in range(8):
        rows = slice(delta * SLOT, (delta + 1) * SLOT)
        for half in range(2):
            kv_out[delta, :, half * PAIR : half * PAIR + 256] = chosen_k[rows, half * 256 : half * 256 + 256]
            kv_out[delta, :, half * PAIR + 256 : half * PAIR + 512] = chosen_v[rows, half * 256 : half * 256 + 256]
            kv_out[delta, :, half * PAIR + 512 : half * PAIR + 640] = chosen_f[rows, :]

    pl.semaphore_wait(pltpu.get_barrier_semaphore(), jnp.where(at_home, 22, 23))

    copies = []

    def start(copy):
        copy.start()
        copies.append(copy)

    def lengths_copy():
        return remote(lengths_ref, len_got, len_send, len_recv, to_device)

    @pl.when(jnp.logical_not(at_home))
    def _():
        lengths_copy().start()

    def out_copy(src, dst, send, recv, width, delta, to_core):
        columns = pl.ds(pl.multiple_of(to_core * width, 128), width)
        slot = delta * 2 + to_core if delta else 0
        return remote(
            src.at[delta, :, columns],
            dst.at[delta, core],
            send.at[slot],
            recv.at[delta, core],
            moved(mine, delta, to_core) if delta else moved(0, 0, other),
        )

    def landed(dst, send, recv, delta, source):
        here = dst.at[delta, source]
        remote(here, here, send.at[0], recv.at[delta, source], moved(0, 0, other)).wait_recv()

    order = (7, 6, 5, 3, 4, 2, 1)
    start(out_copy(kv_out, kv_got, a_send, a_recv, PAIR, 0, other))
    for delta in order:
        for to_core in range(2):
            start(out_copy(kv_out, kv_got, a_send, a_recv, PAIR, delta, to_core))
    own_a = pltpu.make_async_copy(
        kv_out.at[0, :, pl.ds(pl.multiple_of(core * PAIR, 128), PAIR)], kv_got.at[0, core], local_sem.at[0]
    )
    own_a.start()

    for part in range(8):
        columns = slice(part * 512, part * 512 + 512)
        chosen = dot(choose, queries_ref[:, columns]).astype(jnp.bfloat16)
        for delta in range(8):
            q_out[delta, :, columns] = chosen[delta * SLOT : (delta + 1) * SLOT, :]
    start(out_copy(q_out, q_got, q_send, q_recv, HALF, 0, other))
    for delta in order:
        for to_core in range(2):
            start(out_copy(q_out, q_got, q_send, q_recv, HALF, delta, to_core))
    own_q = pltpu.make_async_copy(
        q_out.at[0, :, pl.ds(pl.multiple_of(core * HALF, 128), HALF)], q_got.at[0, core], local_sem.at[1]
    )
    own_q.start()

    own_a.wait()
    landed(kv_got, a_send, a_recv, 0, other)
    for delta in range(1, 8):
        for source in range(2):
            landed(kv_got, a_send, a_recv, delta, source)

    def fields_of(table):
        fields = table.reshape(ROWS, 128).astype(jnp.float32)
        flat = fields.T
        out = []
        for lead, low in ((fields[:, 0:1], fields[:, 1:2]), (flat[0:1, :], flat[1:2, :])):
            lead = lead.astype(jnp.int32)
            out.append((lead > 0, (lead - 1) * 256 + low.astype(jnp.int32)))
        return out

    def holder_of(u):
        block = u >> 8
        return jnp.where(block < 8, block, 15 - block)

    (valid_c, u_c), (valid_r, u_r) = fields_of(kv_got[:, :, :, 512:])
    key_c = jnp.where(valid_c, holder_of(u_c), -1)
    key_r = jnp.where(valid_r, holder_of(u_r), -2)
    key_ref[...] = jnp.broadcast_to(key_c, (ROWS, 128))

    def count_before(step, total):
        base = pl.multiple_of(step * 128, 128)
        chunk = key_ref[pl.ds(base, 128), 0:1]
        hits = (chunk == key_r) & (iota((128, ROWS), 0) + base < iota((128, ROWS), 1))
        return total + jnp.sum(jnp.where(hits, 1, 0), 0, keepdims=True)

    before = lax.fori_loop(0, ROWS // 128, count_before, jnp.zeros((1, ROWS), jnp.int32))
    target = jnp.where(valid_r, key_r * PART + before, -1)

    def fill(step, carry):
        base = pl.multiple_of(step * PART, PART)
        part_out[step] = dot(bf16(iota((PART, ROWS), 0) + base == target), kv_got[...].reshape(ROWS, PAIR)).astype(
            jnp.bfloat16
        )
        return carry

    lax.fori_loop(0, 8, fill, 0)

    def flip(mask):
        out = 0
        for bit in (4, 2, 1):
            digit = place // bit % 2
            out = out + bit * ((1 - digit) if mask & bit else digit)
        return out

    for mask in order:
        start(
            remote(
                part_out.at[flip(mask)], part_got.at[place], b_send.at[mask], b_recv.at[mask], across_cycle(mask)
            )
        )
    part_got[place] = part_out[place]

    index_c, index_r = iota((ROWS, 1), 0), iota((1, ROWS), 1)
    key_c = jnp.where(valid_c, u_c, 4096 + index_c)
    key_r = jnp.where(valid_r, u_r, 4096 + index_r)
    key_ref[...] = jnp.broadcast_to(key_c, (ROWS, 128))

    def rank_step(step, total):
        base = pl.multiple_of(step * 128, 128)
        chunk = key_ref[pl.ds(base, 128), 0:1]
        counts = jnp.sum(jnp.where(key_r < chunk, 1, 0), 1, keepdims=True)
        rank_ref[pl.ds(base, 128), :] = jnp.broadcast_to(counts, (128, 128))
        return total + jnp.sum(jnp.where(chunk < key_r, 1, 0), 0, keepdims=True)

    rank_r = lax.fori_loop(0, ROWS // 128, rank_step, jnp.zeros((1, ROWS), jnp.int32))

    def sort_step(step, total):
        base = pl.multiple_of(step * 128, 128)
        chunk = key_ref[pl.ds(base, 128), 0:1]
        ranks = rank_ref[pl.ds(base, 128), 0:1]
        return total + jnp.sum(jnp.where(ranks == iota((128, ROWS), 1), chunk, 0), 0, keepdims=True)

    sorted_r = lax.fori_loop(0, ROWS // 128, sort_step, jnp.zeros((1, ROWS), jnp.int32))

    @pl.when(at_home)
    def _():
        len_got[...] = lengths_ref[...]

    @pl.when(jnp.logical_not(at_home))
    def _():
        lengths_copy().wait()

    lengths = len_got[...]
    places_ref[0:1, :] = sorted_r
    places_ref[1:2, :] = jnp.where(sorted_r < 4096, document_start(sorted_r, lengths), 8192)
    places_ref[2:8, :] = jnp.zeros((6, ROWS), jnp.int32)

    def turn_step(step, carry):
        base = pl.multiple_of(step * 128, 128)
        hits = iota((128, ROWS), 0) + base == rank_r
        u = jnp.sum(jnp.where(hits, key_r, 0), 1, keepdims=True)
        u = jnp.where(u < 4096, u, 0)
        cos, sin = turning(u - document_start(u, lengths))
        cos_ref[pl.ds(base, 128), :] = cos * SCALE
        sin_ref[pl.ds(base, 128), :] = sin * SCALE
        return carry

    lax.fori_loop(0, ROWS // 128, turn_step, 0)
    rows_c = iota((KEYS, 1), 0)
    key_u = jnp.where(rows_c < BLOCK, place * BLOCK + rows_c, (15 - place) * BLOCK + rows_c - BLOCK)
    key_cos, key_sin = turning(key_u - document_start(key_u, lengths))

    for mask in range(1, 8):
        here = part_got.at[flip(mask)]
        remote(here, here, b_send.at[mask], b_recv.at[mask], across_cycle(mask)).wait_recv()

    _, (valid, u) = fields_of(part_got[:, :, 512:])
    target = jnp.where(valid, jnp.where(u >= 2048, BLOCK, 0) + (u & 255), -1)
    placed = dot(bf16(iota((KEYS, ROWS), 0) == target), part_got[:, :, :512].reshape(ROWS, 512))
    for head in range(2):
        columns = slice(head * HEAD_SIZE, (head + 1) * HEAD_SIZE)
        entry = placed[:, columns]
        entry = entry * key_cos + pltpu.roll(entry, HEAD_SIZE // 2, 1) * key_sin
        own_ref[:, columns] = entry.astype(jnp.bfloat16)
    for half in range(2):
        rows = slice(half * BLOCK, (half + 1) * BLOCK)
        own_ref[rows, 256:] = placed[rows, 256:].T.astype(jnp.bfloat16)

    own_kv = pltpu.make_async_copy(own_ref, all_ref.at[place], local_sem.at[2])
    own_kv.start()

    def kv_copy(third, index):
        start, size, (b1, b2, b3) = THIRDS[third]
        mask, axis = ((0, b1), (0, b2), (0, b3), (b1, b2), (b1, b3), (b2, b3), (b1 ^ b2, b3))[index]
        rows = pl.ds(start, size)
        block = flip(mask)
        src = own_ref.at[rows] if mask == 0 else all_ref.at[block, rows]
        return remote(
            src, all_ref.at[block, rows], kv_send.at[third, index], kv_recv.at[third, index], across_cycle(axis)
        )

    def kv_landed(third, index):
        start, size, (b1, b2, b3) = THIRDS[third]
        mask = (b1, b2, b3, b1 ^ b2, b1 ^ b3, b2 ^ b3, 7)[index]
        here = all_ref.at[flip(mask), pl.ds(start, size)]
        remote(here, here, kv_send.at[third, index], kv_recv.at[third, index], across_cycle(4)).wait_recv()

    for index in range(3):
        for third in range(3):
            start(kv_copy(third, index))

    landed(q_got, q_send, q_recv, 0, other)
    for delta in range(1, 8):
        for source in range(2):
            landed(q_got, q_send, q_recv, delta, source)
    own_q.wait()

    def order_queries(sup):
        base = sup * SUPER
        pick = bf16(iota((SUPER, ROWS), 0) + base == rank_r)
        cos = cos_ref[base : base + SUPER, :]
        sin = sin_ref[base : base + SUPER, :]

        def one_part(part, carry):
            columns = pl.ds(pl.multiple_of(part * 256, 256), 256)
            rows = dot(pick, q_got[:, :, :, columns].reshape(ROWS, 256))
            for one in range(2):
                entry = rows[:, one * HEAD_SIZE : (one + 1) * HEAD_SIZE]
                entry = entry * cos + pltpu.roll(entry, HEAD_SIZE // 2, 1) * sin
                entry = entry.astype(jnp.bfloat16)
                first = pl.multiple_of((part % 4 * 2 + one) * TILE, TILE)
                for tile in range(SUPER // TILE):
                    sorted_ref[part // 4, sup * (SUPER // TILE) + tile, pl.ds(first, TILE), :] = entry[
                        tile * TILE : (tile + 1) * TILE
                    ]
            return carry

        lax.fori_loop(0, 8, one_part, 0)

    for third in range(3):
        kv_landed(third, 0)
        start(kv_copy(third, 3))
        start(kv_copy(third, 4))
    for third in range(3):
        kv_landed(third, 1)
        start(kv_copy(third, 5))
    order_queries(0)
    for third in range(3):
        kv_landed(third, 3)
        start(kv_copy(third, 6))
    for sup in range(1, 4):
        order_queries(sup)
    for index in (2, 4, 5, 6):
        for third in range(3):
            kv_landed(third, index)
    own_kv.wait()
    for copy in copies:
        copy.wait_send()


def across_cycle(mask):
    x, y, z, core = coords()
    return device(x + 2 * (mask // 4), y + 2 * (mask // 2 % 2), z + 2 * (mask % 2), core)


def exchange(queries, keys, values, plan_col, plan_row, lengths):
    vmem = pl.BlockSpec(memory_space=pltpu.VMEM)
    dma = pltpu.SemaphoreType.DMA
    return pl.pallas_call(
        exchange_kernel,
        out_shape=(
            jax.ShapeDtypeStruct((2, ROWS // TILE, TILE * 8, HEAD_SIZE), jnp.bfloat16),
            jax.ShapeDtypeStruct((8, KEYS, 512), jnp.bfloat16),
            jax.ShapeDtypeStruct((8, ROWS), jnp.int32),
            jax.ShapeDtypeStruct((ROWS, 128), jnp.int32),
        ),
        in_specs=[vmem] * 6,
        out_specs=[vmem, pl.BlockSpec(memory_space=pl.ANY), vmem, vmem],
        scratch_shapes=[
            pltpu.VMEM((8, SLOT, 2 * HALF), jnp.bfloat16),
            pltpu.VMEM((8, 2, SLOT, HALF), jnp.bfloat16),
            pltpu.VMEM((8, SLOT, 2 * PAIR), jnp.bfloat16),
            pltpu.VMEM((8, 2, SLOT, PAIR), jnp.bfloat16),
            pltpu.VMEM((8, PART, PAIR), jnp.bfloat16),
            pltpu.VMEM((8, PART, PAIR), jnp.bfloat16),
            pltpu.VMEM((KEYS, 512), jnp.bfloat16),
            pltpu.VMEM((8, 128), jnp.int32),
            pltpu.VMEM((ROWS, 128), jnp.int32),
            pltpu.VMEM((ROWS, HEAD_SIZE), jnp.float32),
            pltpu.VMEM((ROWS, HEAD_SIZE), jnp.float32),
            dma((16,)), dma((8, 2)), dma((16,)), dma((8, 2)), dma((8,)), dma((8,)), dma((3, 7)), dma((3, 7)),
            dma(()), dma(()), dma((3,)),
        ],
        compiler_params=pltpu.CompilerParams(
            collective_id=0, has_side_effects=True, vmem_limit_bytes=VMEM_LIMIT
        ),
        name="exchange",
    )(queries, keys, values, plan_col, plan_row, lengths)


def back_kernel(
    made_ref, rank_ref, plan_col, plan_row, out_ref, send_ref, ret_ref, send, recv, local_sem
):
    x, y, z, core = coords()
    my_cycle = x % 2 * 4 + y % 2 * 2 + z % 2
    mine = sign_of(core)
    other = 1 - core
    for delta in range(1, 8):
        for worker in range(2):
            signal(moved(mine, delta, worker))
    signal(moved(0, 0, other))

    columns = pl.ds(pl.multiple_of(core * HALF, 128), HALF)

    def place_rows(first):
        rows = slice(first * 2 * SLOT, first * 2 * SLOT + 4 * SLOT)
        put = bf16(rank_ref[rows, 0:1] == iota((4 * SLOT, ROWS), 1))

        def one_part(part, carry):
            here = pl.ds(pl.multiple_of(part * 512, 512), 512)
            chosen = dot(put, made_ref[:, here]).astype(jnp.bfloat16)
            for one in range(4):
                send_ref[first + one // 2, one % 2, :, here] = chosen[one * SLOT : (one + 1) * SLOT, :]
            return carry

        lax.fori_loop(0, 4, one_part, 0)

    copies = []

    def start(delta, source):
        copy = remote(
            send_ref.at[delta, source],
            ret_ref.at[delta, :, columns],
            send.at[delta * 2 + source],
            recv.at[delta, core],
            moved(-sign_of(source), delta, source),
        )
        copy.start()
        copies.append(copy)

    place_rows(6)
    pl.semaphore_wait(pltpu.get_barrier_semaphore(), 15)
    for first in (6, 4, 2, 0):
        if first < 6:
            place_rows(first)
        for delta in (first + 1, first):
            if delta:
                for source in range(2):
                    start(delta, source)
    own = pltpu.make_async_copy(send_ref.at[0, core], ret_ref.at[0, :, columns], local_sem)
    own.start()
    copy = remote(
        send_ref.at[0, other], ret_ref.at[0, :, columns], send.at[0], recv.at[0, core], moved(0, 0, other)
    )
    copy.start()
    copies.append(copy)

    plan_c, plan_r = plan_col[...], plan_row[...]
    same = (cycle_of(plan_c) == cycle_of(plan_r)) & (iota((TOK, TOK), 1) < iota((TOK, TOK), 0))
    rank = jnp.sum(jnp.where(same, 1, 0), 1, keepdims=True)
    row = jnp.bitwise_xor(cycle_of(plan_c), my_cycle) * SLOT + rank
    choose = bf16(iota((TOK, 8 * SLOT), 1) == row)

    def landed(delta, worker):
        here = ret_ref.at[delta, :, pl.ds(pl.multiple_of(worker * HALF, 128), HALF)]
        remote(here, here, send.at[0], recv.at[delta, worker], moved(0, 0, other)).wait_recv()

    own.wait()
    landed(0, other)
    for delta in range(1, 8):
        for worker in range(2):
            landed(delta, worker)

    def finish(part, carry):
        here = pl.ds(pl.multiple_of(part * 512, 512), 512)
        out_ref[:, here] = dot(choose, ret_ref[:, :, here].reshape(8 * SLOT, 512)).astype(jnp.bfloat16)
        return carry

    lax.fori_loop(0, 8, finish, 0)
    for copy in copies:
        copy.wait_send()


def back(made, rank, plan_col, plan_row):
    vmem = pl.BlockSpec(memory_space=pltpu.VMEM)
    return pl.pallas_call(
        back_kernel,
        out_shape=jax.ShapeDtypeStruct((TOK, 2 * HALF), jnp.bfloat16),
        in_specs=[vmem] * 4,
        out_specs=vmem,
        scratch_shapes=[
            pltpu.VMEM((8, 2, SLOT, HALF), jnp.bfloat16),
            pltpu.VMEM((8, SLOT, 2 * HALF), jnp.bfloat16),
            pltpu.SemaphoreType.DMA((16,)),
            pltpu.SemaphoreType.DMA((8, 2)),
            pltpu.SemaphoreType.DMA(()),
        ],
        compiler_params=pltpu.CompilerParams(
            collective_id=1, has_side_effects=True, vmem_limit_bytes=VMEM_LIMIT
        ),
        name="back",
    )(made, rank, plan_col, plan_row)


def attend_kernel(
    low_ref, high_ref, u_ref, begin_ref, turned, kv_ref,
    made, peak, total, summed, decays, scores0, scores1, weights0, weights1,
):
    across = iota((BLOCK, TILE * 8), 0)

    def one_tile(tile, carry):
        low = low_ref[tile]
        high = high_ref[tile]
        there = pl.multiple_of(tile * TILE, TILE)

        @pl.when(high < low)
        def _():
            made[pl.ds(there, TILE), :] = jnp.zeros((TILE, HALF), jnp.bfloat16)

        @pl.when(high >= low)
        def _():
            live_tile(tile, low, high, there)

        return carry

    def live_tile(tile, low, high, there):
        begin = begin_ref[pl.ds(tile, 1), :]
        last = u_ref[pl.ds(tile, 1), :]
        peak[...] = jnp.full_like(peak, NEG)
        summed[...] = jnp.zeros_like(summed)
        total[...] = jnp.zeros_like(total)
        decays[...] = jnp.ones_like(decays)
        weights1[...] = jnp.zeros_like(weights1)

        def spot(block):
            block = jnp.minimum(block, 15)
            return jnp.where(block < 8, block, 15 - block), jnp.where(block < 8, 0, BLOCK)

        def score_of(block, scores):
            holder, row = spot(block)
            place = across + block * BLOCK
            allowed = (place >= begin) & (place <= last)
            for head in range(2):
                key = kv_ref[
                    holder,
                    pl.ds(pl.multiple_of(row, BLOCK), BLOCK),
                    head * HEAD_SIZE : (head + 1) * HEAD_SIZE,
                ]
                score = lax.dot_general(
                    key, turned[head, tile], (((1,), (1,)), ((), ())), preferred_element_type=jnp.float32
                )
                scores[head] = jnp.where(allowed, score, NEG)

        def weigh(scores, weights, head):
            score = scores[head]
            old = peak[head]
            new = jnp.maximum(old, jnp.max(score, 0, keepdims=True))
            decay = jnp.exp2(old - new)
            peak[head] = new
            weight = jnp.exp2(score - new)
            summed[head] = summed[head] * decay + jnp.sum(weight, 0, keepdims=True)
            weights[head] = weight.astype(jnp.bfloat16)
            decays[head] = decay

        def add(block, weights, head):
            holder, row = spot(block)
            value = kv_ref[
                holder,
                pl.ds(pl.multiple_of(row + head * HEAD_SIZE, HEAD_SIZE), HEAD_SIZE),
                2 * HEAD_SIZE :,
            ]
            total[head] = total[head] * decays[head] + jnp.dot(
                value, weights[head], preferred_element_type=jnp.float32
            )

        score_of(low, scores0)

        def one_step(step, carry):
            block = low + step * 2
            for head in range(2):
                add(jnp.maximum(block - 1, 0), weights1, head)
            score_of(block + 1, scores1)
            for head in range(2):
                weigh(scores0, weights0, head)
            for head in range(2):
                add(block, weights0, head)
            score_of(block + 2, scores0)
            for head in range(2):
                weigh(scores1, weights1, head)
            return carry

        steps = (high - low + 2) // 2
        lax.fori_loop(0, steps, one_step, 0)
        for head in range(2):
            add(jnp.maximum(low + steps * 2 - 1, 0), weights1, head)
        for head in range(2):
            result = (total[head] / jnp.maximum(summed[head], 1e-30)).T.astype(jnp.bfloat16)
            for one in range(8):
                made[pl.ds(there, TILE), pl.ds((head * 8 + one) * HEAD_SIZE, HEAD_SIZE)] = result[
                    one * TILE : (one + 1) * TILE
                ]

    lax.fori_loop(0, ROWS // TILE, one_tile, 0)


def per_tile(column):
    return jnp.tile(column.reshape(ROWS // TILE, TILE), (1, 8))


def attend(low, high, u, begin, q, kv):
    smem = pl.BlockSpec(memory_space=pltpu.SMEM)
    vmem = pl.BlockSpec(memory_space=pltpu.VMEM)
    lanes = TILE * 8
    return pl.pallas_call(
        attend_kernel,
        out_shape=jax.ShapeDtypeStruct((ROWS, HALF), jnp.bfloat16),
        in_specs=[smem] * 2 + [vmem] * 4,
        out_specs=vmem,
        scratch_shapes=[
            pltpu.VMEM((2, 1, lanes), jnp.float32),
            pltpu.VMEM((2, HEAD_SIZE, lanes), jnp.float32),
            pltpu.VMEM((2, 1, lanes), jnp.float32),
            pltpu.VMEM((2, 1, lanes), jnp.float32),
            pltpu.VMEM((2, BLOCK, lanes), jnp.float32),
            pltpu.VMEM((2, BLOCK, lanes), jnp.float32),
            pltpu.VMEM((2, BLOCK, lanes), jnp.bfloat16),
            pltpu.VMEM((2, BLOCK, lanes), jnp.bfloat16),
        ],
        compiler_params=pltpu.CompilerParams(vmem_limit_bytes=VMEM_LIMIT),
        name="attend",
    )(low, high, per_tile(u), per_tile(begin), q, kv)


def local(queries, keys, values, plan, doc_lengths):
    plan_col, plan_row = plan[:, None], plan[None, :]
    lengths = jnp.pad(doc_lengths, ((0, 7), (0, 124)))
    q, kv, places, rank = exchange(queries, keys, values, plan_col, plan_row, lengths)
    u, begin = places[0], places[1]
    live = u < 4096
    low = jnp.where(live, begin // BLOCK, 0).reshape(ROWS // TILE, TILE)[:, 0]
    high = jnp.max(jnp.where(live, u // BLOCK, -1).reshape(ROWS // TILE, TILE), 1)
    made = attend(low, high, u, begin, q, kv)
    return back(made, rank, plan_col, plan_row)


def solution(mesh):
    return jax.shard_map(
        local,
        mesh=mesh,
        in_specs=(
            P(("blk", "group"), None),
            P(("blk", "group"), None),
            P(("blk", "group"), None),
            P(("blk", "group")),
            P("group", None),
        ),
        out_specs=P(("blk", "group"), None),
        check_vma=False,
    )
```

time: 214 us -> 185 us (0.86)
  Pallas kernels: 150 us -> 175 us
  waiting for transfers between devices: 17.6 us -> 0 us
  other arithmetic: 18 us -> 1.22 us
  starting transfers between devices: 11.5 us -> 0 us
  matrix products: 10.3 us -> 0 us
  local copies, waits for them, and re-layouts: 5.25 us -> 8.42 us
    pallas_call x2, Pallas kernels: 101 us -> 145 us  [the longest x1 84.3 us: exchange(): pl.pallas_call(exchange_kernel, out_shape=(jax.ShapeDtypeStruct((2, ROWS...]
    pallas_call x1, Pallas kernels: 49 us -> 30 us  [attend(): pl.pallas_call(attend_kernel, out_shape=jax.ShapeDtypeStruct((ROWS, HALF)...]
    all_to_all x1 -> x0, waiting for transfers between devices: 17.6 us -> none  [local(): lax.all_to_all(jnp.concatenate(halves, 1).reshape(128, 8, 640), ('blk', '...]
    all_to_all x1 -> x0, starting transfers between devices: 11.5 us -> none  [local(): lax.all_to_all(jnp.concatenate(halves, 1).reshape(128, 8, 640), ('blk', '...]
    dot_general x5 -> x0, matrix products: 10.3 us -> none  [the longest x1 4.81 us: local(): lax.dot_general(send_q, ret, (((0,), (0,)), ((), ())), preferred_element_...]
    select_n x5 -> x0, other arithmetic: 3.5 us -> none  [the longest x1 1.56 us: local(): sort_key = jnp.where(valid, u, 4096 + index)]
    another operation x9 -> x0, other arithmetic: 2.24 us -> none
    reduce_sum x7 -> x0, other arithmetic: 2.22 us -> none  [the longest x1 0.63 us: local(): count = jnp.sum(valid.astype(jnp.int32))]
  transfers between devices with their start and end apart: 1 -> 0, of which waited for: 1 -> 0; matrix products, arithmetic and copies ran while one was open for 2% -> 0% of each run, Pallas kernels for 0% -> 0%
where the time goes in v2:
time: 185 us
  Pallas kernels  175 us (95%)
  local copies, waits for them, and re-layouts  8.42 us (5%)
    pallas_call x1, Pallas kernels, exchange(): pl.pallas_call(exchange_kernel, out_shape=(jax.ShapeDtypeStruct((2, ROWS...  84.3 us
    pallas_call x1, Pallas kernels, back(): pl.pallas_call(back_kernel, out_shape=jax.ShapeDtypeStruct((TOK, 2 * HALF...  61.1 us
    pallas_call x1, Pallas kernels, attend(): pl.pallas_call(attend_kernel, out_shape=jax.ShapeDtypeStruct((ROWS, HALF)...  30 us

profile of v2, /device:TPU:1, one launch (start us, length us, event | category | flops | bytes accessed | tf_op | source)
XLA Modules:
  0.0 185.2 jit_solution(14819443608361551906)
XLA Ops:
  0.0 1.3 pad.4.lengths_ref
  1.3 1.5 copy.15.plan_col
  2.7 84.3 %exchange.1 = (bf16[2,32,256,128]{3,2,1,0:T(8,128)(2,1)}, bf16[8,512,512]{2,1,0:T(8,128)(2,1)}, s32[8,1024]{1,0:T(8,128)}, s32[1024,128]{1,0:T(8,128)}) custom-call(bf16[256,4096]{1,0:T(8,128)(2,1)} %queries_ref.1, bf16[256,512]{1,0:T(8,128)(2,1)} %keys_ref.1, bf16[256,512]{1,0:T(8,128)(2,1)} %values_ref.1, s32[256,1]{1,0:T(8,128)} %copy.15.plan_col, ...), custom_call_target="tpu_custom_call" | custom-call | tf_op jit(solution)/shard_map/exchange/pallas_call | solution.py:416
  87.1 0.9 slice_reduce_fusion
  87.9 0.1 squeeze.10
  88.0 0.1 copy.17
  88.1 0.1 squeeze.9
  88.1 0.1 copy.16
  88.2 0.6 fusion.2.high_ref
  88.8 0.6 fusion.4.low_ref
  89.5 0.7 tile.17.u_ref
  90.2 0.7 tile.19.begin_ref
  90.9 30.0 %attend.1.made_ref = bf16[1024,2048]{1,0:T(8,128)(2,1)} custom-call(s32[32]{0:T(128)} %fusion.4.low_ref, s32[32]{0:T(128)} %fusion.2.high_ref, s32[32,256]{1,0:T(8,128)} %tile.17.u_ref, s32[32,256]{1,0:T(8,128)} %tile.19.begin_ref, bf16[2,32,256,128]{3,2,1,0:T(8,128)(2,1)} %get-tuple-element.10.turned, bf16[8,512,512]{2,1,0:T(8,128)(2,1)} %get-tuple-element.11.kv_ref), custom_call_target="tpu_custom_call" | custom-call | tf_op jit(solution)/shard_map/attend/pallas_call | solution.py:661
  120.9 61.1 %back.1 = bf16[256,4096]{1,0:T(8,128)(2,1)} custom-call(bf16[1024,2048]{1,0:T(8,128)(2,1)} %attend.1.made_ref, s32[1024,128]{1,0:T(8,128)} %get-tuple-element.12.rank_ref, s32[256,1]{1,0:T(8,128)} %copy.15.plan_col, s32[1,256]{1,0:T(1,128)} %bitcast.6), custom_call_target="tpu_custom_call" | custom-call | tf_op jit(solution)/shard_map/back/pallas_call | solution.py:533
  182.0 3.1 %copy.27 = bf16[256,4096]{1,0:T(8,128)(2,1)} copy(bf16[256,4096]{1,0:T(8,128)(2,1)} %back.1) | data formatting | bytes 4194304
  (4 shorter events, 0.0 us)

commit v3 on v2

--- a/solution.py
+++ b/solution.py
@@ -84,6 +84,11 @@
     return jnp.where(offset < 128, p * 128 + offset, (31 - p) * 128 + offset - 128)
 
 
+def column_of(row):
+    size = row.shape[1]
+    return jnp.sum(jnp.where(iota((size, size), 0) == iota((size, size), 1), row, 0), 1, keepdims=True)
+
+
 def document_start(u, lengths):
     end = jnp.zeros((1, 1), jnp.int32)
     start = jnp.zeros_like(u)
@@ -107,10 +112,10 @@
 
 
 def exchange_kernel(
-    queries_ref, keys_ref, values_ref, plan_col, plan_row, lengths_ref,
-    sorted_ref, all_ref, places_ref, rank_ref,
-    q_out, q_got, kv_out, kv_got, part_out, part_got, own_ref, len_got, key_ref, cos_ref, sin_ref,
-    q_send, q_recv, a_send, a_recv, b_send, b_recv, kv_send, kv_recv, len_send, len_recv, local_sem,
+    queries_ref, keys_ref, values_ref, plan_row, lengths_ref,
+    turned_ref, all_ref, last_ref, begin_ref, bounds_ref, rank_ref,
+    q_out, q_got, kv_out, kv_got, part_out, part_got, own_ref, len_out, len_got, key_ref, cos_ref, sin_ref, sorted_ref,
+    q_send, q_recv, a_send, a_recv, b_send, b_recv, kv_send, kv_recv, len_send, len_recv, local_sem, out_sem,
 ):
     x, y, z, core = coords()
     place = x // 2 * 4 + y // 2 * 2 + z // 2
@@ -137,7 +142,10 @@
     def _():
         signal((from_block, my_cycle))
 
-    plan_c, plan_r = plan_col[...], plan_row[...]
+    len_out[...] = jnp.zeros_like(len_out)
+    len_out[0:1, 0:4] = lengths_ref[...]
+    plan_r = plan_row[...]
+    plan_c = column_of(plan_r)
     same = (cycle_of(plan_c) == cycle_of(plan_r)) & (iota((TOK, TOK), 0) < iota((TOK, TOK), 1))
     rank = jnp.sum(jnp.where(same, 1, 0), 0, keepdims=True)
     row = jnp.bitwise_xor(cycle_of(plan_r), my_cycle) * SLOT + rank
@@ -165,7 +173,7 @@
         copies.append(copy)
 
     def lengths_copy():
-        return remote(lengths_ref, len_got, len_send, len_recv, to_device)
+        return remote(len_out, len_got, len_send, len_recv, to_device)
 
     @pl.when(jnp.logical_not(at_home))
     def _():
@@ -202,9 +210,21 @@
         for delta in range(8):
             q_out[delta, :, columns] = chosen[delta * SLOT : (delta + 1) * SLOT, :]
     start(out_copy(q_out, q_got, q_send, q_recv, HALF, 0, other))
+    for chunk in range(SLOT // 16):
+        for delta in order:
+            for to_core in range(2):
+                columns = pl.ds(to_core * HALF, HALF)
+                rows = pl.ds(chunk * 16, 16)
+                remote(
+                    q_out.at[delta, rows, columns],
+                    q_got.at[delta, core, rows],
+                    q_send.at[delta * 2 + to_core],
+                    q_recv.at[delta, core],
+                    moved(mine, delta, to_core),
+                ).start()
     for delta in order:
         for to_core in range(2):
-            start(out_copy(q_out, q_got, q_send, q_recv, HALF, delta, to_core))
+            copies.append(out_copy(q_out, q_got, q_send, q_recv, HALF, delta, to_core))
     own_q = pltpu.make_async_copy(
         q_out.at[0, :, pl.ds(pl.multiple_of(core * HALF, 128), HALF)], q_got.at[0, core], local_sem.at[1]
     )
@@ -244,13 +264,12 @@
     target = jnp.where(valid_r, key_r * PART + before, -1)
 
     def fill(step, carry):
-        base = pl.multiple_of(step * PART, PART)
-        part_out[step] = dot(bf16(iota((PART, ROWS), 0) + base == target), kv_got[...].reshape(ROWS, PAIR)).astype(
-            jnp.bfloat16
-        )
+        base = pl.multiple_of(step * 4 * PART, 4 * PART)
+        rows = dot(bf16(iota((4 * PART, ROWS), 0) + base == target), kv_got[...].reshape(ROWS, PAIR))
+        part_out[pl.ds(step * 4, 4)] = rows.astype(jnp.bfloat16).reshape(4, PART, PAIR)
         return carry
 
-    lax.fori_loop(0, 8, fill, 0)
+    lax.fori_loop(0, 2, fill, 0)
 
     def flip(mask):
         out = 0
@@ -291,28 +310,47 @@
 
     @pl.when(at_home)
     def _():
-        len_got[...] = lengths_ref[...]
+        len_got[...] = len_out[...]
 
     @pl.when(jnp.logical_not(at_home))
     def _():
         lengths_copy().wait()
 
     lengths = len_got[...]
-    places_ref[0:1, :] = sorted_r
-    places_ref[1:2, :] = jnp.where(sorted_r < 4096, document_start(sorted_r, lengths), 8192)
-    places_ref[2:8, :] = jnp.zeros((6, ROWS), jnp.int32)
+    begin_r = jnp.where(sorted_r < 4096, document_start(sorted_r, lengths), 8192)
+
+    own_tile = iota((ROWS // TILE, ROWS), 1) >> 5 == iota((ROWS // TILE, ROWS), 0)
+    spread = bf16(iota((ROWS, TILE * 8), 0) & (TILE - 1) == iota((ROWS, TILE * 8), 1) & (TILE - 1))
+    for values, tiles_ref in ((sorted_r, last_ref), (begin_r, begin_ref)):
+        parts = [
+            dot(jnp.where(own_tile, half, 0).astype(jnp.float32).astype(jnp.bfloat16), spread).astype(jnp.int32)
+            for half in (values >> 8, values & 255)
+        ]
+        tiles_ref[...] = parts[0] * 256 + parts[1]
 
     def turn_step(step, carry):
+        low, high = carry
         base = pl.multiple_of(step * 128, 128)
         hits = iota((128, ROWS), 0) + base == rank_r
         u = jnp.sum(jnp.where(hits, key_r, 0), 1, keepdims=True)
-        u = jnp.where(u < 4096, u, 0)
-        cos, sin = turning(u - document_start(u, lengths))
+        live = u < 4096
+        start = document_start(u, lengths)
+        index, tile = iota((128, 128), 0) + base, iota((128, 128), 1)
+        low = low + jnp.sum(jnp.where((index == tile * TILE) & live, start >> 8, 0), 0, keepdims=True)
+        high = jnp.maximum(
+            high, jnp.max(jnp.where((index >> 5 == tile) & live, u >> 8, -1), 0, keepdims=True)
+        )
+        cos, sin = turning(jnp.where(live, u - start, 0))
         cos_ref[pl.ds(base, 128), :] = cos * SCALE
         sin_ref[pl.ds(base, 128), :] = sin * SCALE
-        return carry
-
-    lax.fori_loop(0, ROWS // 128, turn_step, 0)
+        return low, high
+
+    low, high = lax.fori_loop(
+        0, ROWS // 128, turn_step, (jnp.zeros((1, 128), jnp.int32), jnp.full((1, 128), -1, jnp.int32))
+    )
+    bounds_ref[...] = jnp.zeros_like(bounds_ref)
+    bounds_ref[0:1, :] = low
+    bounds_ref[1:2, :] = high
     rows_c = iota((KEYS, 1), 0)
     key_u = jnp.where(rows_c < BLOCK, place * BLOCK + rows_c, (15 - place) * BLOCK + rows_c - BLOCK)
     key_cos, key_sin = turning(key_u - document_start(key_u, lengths))
@@ -383,6 +421,11 @@
             return carry
 
         lax.fori_loop(0, 8, one_part, 0)
+        turned_copy(sup).start()
+
+    def turned_copy(sup):
+        tiles = pl.ds(sup * (SUPER // TILE), SUPER // TILE)
+        return pltpu.make_async_copy(sorted_ref.at[:, tiles], turned_ref.at[:, tiles], out_sem.at[sup])
 
     for third in range(3):
         kv_landed(third, 0)
@@ -401,6 +444,8 @@
         for third in range(3):
             kv_landed(third, index)
     own_kv.wait()
+    for sup in range(4):
+        turned_copy(sup).wait()
     for copy in copies:
         copy.wait_send()
 
@@ -410,7 +455,7 @@
     return device(x + 2 * (mask // 4), y + 2 * (mask // 2 % 2), z + 2 * (mask % 2), core)
 
 
-def exchange(queries, keys, values, plan_col, plan_row, lengths):
+def exchange(queries, keys, values, plan_row, lengths):
     vmem = pl.BlockSpec(memory_space=pltpu.VMEM)
     dma = pltpu.SemaphoreType.DMA
     return pl.pallas_call(
@@ -418,11 +463,13 @@
         out_shape=(
             jax.ShapeDtypeStruct((2, ROWS // TILE, TILE * 8, HEAD_SIZE), jnp.bfloat16),
             jax.ShapeDtypeStruct((8, KEYS, 512), jnp.bfloat16),
-            jax.ShapeDtypeStruct((8, ROWS), jnp.int32),
+            jax.ShapeDtypeStruct((ROWS // TILE, TILE * 8), jnp.int32),
+            jax.ShapeDtypeStruct((ROWS // TILE, TILE * 8), jnp.int32),
+            jax.ShapeDtypeStruct((8, 128), jnp.int32),
             jax.ShapeDtypeStruct((ROWS, 128), jnp.int32),
         ),
-        in_specs=[vmem] * 6,
-        out_specs=[vmem, pl.BlockSpec(memory_space=pl.ANY), vmem, vmem],
+        in_specs=[vmem] * 5,
+        out_specs=[pl.BlockSpec(memory_space=pl.ANY)] * 2 + [vmem] * 4,
         scratch_shapes=[
             pltpu.VMEM((8, SLOT, 2 * HALF), jnp.bfloat16),
             pltpu.VMEM((8, 2, SLOT, HALF), jnp.bfloat16),
@@ -432,24 +479,23 @@
             pltpu.VMEM((8, PART, PAIR), jnp.bfloat16),
             pltpu.VMEM((KEYS, 512), jnp.bfloat16),
             pltpu.VMEM((8, 128), jnp.int32),
+            pltpu.VMEM((8, 128), jnp.int32),
             pltpu.VMEM((ROWS, 128), jnp.int32),
             pltpu.VMEM((ROWS, HEAD_SIZE), jnp.float32),
             pltpu.VMEM((ROWS, HEAD_SIZE), jnp.float32),
+            pltpu.VMEM((2, ROWS // TILE, TILE * 8, HEAD_SIZE), jnp.bfloat16),
             dma((16,)), dma((8, 2)), dma((16,)), dma((8, 2)), dma((8,)), dma((8,)), dma((3, 7)), dma((3, 7)),
-            dma(()), dma(()), dma((3,)),
+            dma(()), dma(()), dma((3,)), dma((4,)),
         ],
         compiler_params=pltpu.CompilerParams(
             collective_id=0, has_side_effects=True, vmem_limit_bytes=VMEM_LIMIT
         ),
         name="exchange",
-    )(queries, keys, values, plan_col, plan_row, lengths)
-
-
-def back_kernel(
-    made_ref, rank_ref, plan_col, plan_row, out_ref, send_ref, ret_ref, send, recv, local_sem
-):
+    )(queries, keys, values, plan_row, lengths)
+
+
+def back_kernel(made_ref, rank_ref, ret_ref, send_ref, send, recv, local_sem):
     x, y, z, core = coords()
-    my_cycle = x % 2 * 4 + y % 2 * 2 + z % 2
     mine = sign_of(core)
     other = 1 - core
     for delta in range(1, 8):
@@ -474,26 +520,29 @@
 
     copies = []
 
-    def start(delta, source):
-        copy = remote(
-            send_ref.at[delta, source],
-            ret_ref.at[delta, :, columns],
+    def back_copy(delta, source, first, size):
+        rows = pl.ds(first, size)
+        return remote(
+            send_ref.at[delta, source, rows],
+            ret_ref.at[delta, rows, columns],
             send.at[delta * 2 + source],
             recv.at[delta, core],
             moved(-sign_of(source), delta, source),
         )
-        copy.start()
-        copies.append(copy)
 
     place_rows(6)
     pl.semaphore_wait(pltpu.get_barrier_semaphore(), 15)
     for first in (6, 4, 2, 0):
         if first < 6:
             place_rows(first)
-        for delta in (first + 1, first):
-            if delta:
+        deltas = [delta for delta in (first + 1, first) if delta]
+        for chunk in range(SLOT // 16):
+            for delta in deltas:
                 for source in range(2):
-                    start(delta, source)
+                    back_copy(delta, source, chunk * 16, 16).start()
+        for delta in deltas:
+            for source in range(2):
+                copies.append(back_copy(delta, source, 0, SLOT))
     own = pltpu.make_async_copy(send_ref.at[0, core], ret_ref.at[0, :, columns], local_sem)
     own.start()
     copy = remote(
@@ -502,12 +551,6 @@
     copy.start()
     copies.append(copy)
 
-    plan_c, plan_r = plan_col[...], plan_row[...]
-    same = (cycle_of(plan_c) == cycle_of(plan_r)) & (iota((TOK, TOK), 1) < iota((TOK, TOK), 0))
-    rank = jnp.sum(jnp.where(same, 1, 0), 1, keepdims=True)
-    row = jnp.bitwise_xor(cycle_of(plan_c), my_cycle) * SLOT + rank
-    choose = bf16(iota((TOK, 8 * SLOT), 1) == row)
-
     def landed(delta, worker):
         here = ret_ref.at[delta, :, pl.ds(pl.multiple_of(worker * HALF, 128), HALF)]
         remote(here, here, send.at[0], recv.at[delta, worker], moved(0, 0, other)).wait_recv()
@@ -518,26 +561,19 @@
         for worker in range(2):
             landed(delta, worker)
 
-    def finish(part, carry):
-        here = pl.ds(pl.multiple_of(part * 512, 512), 512)
-        out_ref[:, here] = dot(choose, ret_ref[:, :, here].reshape(8 * SLOT, 512)).astype(jnp.bfloat16)
-        return carry
-
-    lax.fori_loop(0, 8, finish, 0)
     for copy in copies:
         copy.wait_send()
 
 
-def back(made, rank, plan_col, plan_row):
+def back(made, rank):
     vmem = pl.BlockSpec(memory_space=pltpu.VMEM)
     return pl.pallas_call(
         back_kernel,
-        out_shape=jax.ShapeDtypeStruct((TOK, 2 * HALF), jnp.bfloat16),
-        in_specs=[vmem] * 4,
-        out_specs=vmem,
+        out_shape=jax.ShapeDtypeStruct((8, SLOT, 2 * HALF), jnp.bfloat16),
+        in_specs=[vmem] * 2,
+        out_specs=pl.BlockSpec(memory_space=pl.ANY),
         scratch_shapes=[
             pltpu.VMEM((8, 2, SLOT, HALF), jnp.bfloat16),
-            pltpu.VMEM((8, SLOT, 2 * HALF), jnp.bfloat16),
             pltpu.SemaphoreType.DMA((16,)),
             pltpu.SemaphoreType.DMA((8, 2)),
             pltpu.SemaphoreType.DMA(()),
@@ -546,18 +582,62 @@
             collective_id=1, has_side_effects=True, vmem_limit_bytes=VMEM_LIMIT
         ),
         name="back",
-    )(made, rank, plan_col, plan_row)
+    )(made, rank)
+
+
+def restore_kernel(cycle_ref, plan_row, ret_ref, out_ref, choose_ref):
+    @pl.when(pl.program_id(0) == 0)
+    def _():
+        plan_r = plan_row[...]
+        plan_c = column_of(plan_r)
+        same = (cycle_of(plan_c) == cycle_of(plan_r)) & (iota((TOK, TOK), 1) < iota((TOK, TOK), 0))
+        rank = jnp.sum(jnp.where(same, 1, 0), 1, keepdims=True)
+        row = jnp.bitwise_xor(cycle_of(plan_c), cycle_ref[0]) * SLOT + rank
+        choose_ref[...] = bf16(iota((TOK, 8 * SLOT), 1) == row)
+
+    rows = ret_ref[...].reshape(8 * SLOT, ret_ref.shape[2])
+    out_ref[...] = dot(choose_ref[...], rows).astype(jnp.bfloat16)
+
+
+def restore(my_cycle, plan_row, ret):
+    width = 1024
+    return pl.pallas_call(
+        restore_kernel,
+        grid=(2 * HALF // width,),
+        out_shape=jax.ShapeDtypeStruct((TOK, 2 * HALF), jnp.bfloat16),
+        in_specs=[
+            pl.BlockSpec(memory_space=pltpu.SMEM),
+            pl.BlockSpec((1, TOK), lambda i: (0, 0)),
+            pl.BlockSpec((8, SLOT, width), lambda i: (0, 0, i)),
+        ],
+        out_specs=pl.BlockSpec((TOK, width), lambda i: (0, i)),
+        scratch_shapes=[pltpu.VMEM((TOK, 8 * SLOT), jnp.bfloat16)],
+        compiler_params=pltpu.CompilerParams(vmem_limit_bytes=VMEM_LIMIT),
+        name="restore",
+    )(my_cycle, plan_row, ret)
 
 
 def attend_kernel(
-    low_ref, high_ref, u_ref, begin_ref, turned, kv_ref,
-    made, peak, total, summed, decays, scores0, scores1, weights0, weights1,
+    bounds_ref, last_ref, begin_ref, turned_ref, kv_ref,
+    made_ref, turned, made, peak, total, summed, decays, scores0, scores1, weights0, weights1, in_sem, out_sem,
 ):
     across = iota((BLOCK, TILE * 8), 0)
+    group = SUPER // TILE
+
+    def load(sup):
+        tiles = pl.ds(sup * group, group)
+        return pltpu.make_async_copy(turned_ref.at[:, tiles], turned.at[:, tiles], in_sem.at[sup])
+
+    def store(sup):
+        rows = pl.ds(sup * SUPER, SUPER)
+        return pltpu.make_async_copy(made.at[rows], made_ref.at[rows], out_sem.at[sup])
+
+    for sup in range(ROWS // SUPER):
+        load(sup).start()
 
     def one_tile(tile, carry):
-        low = low_ref[tile]
-        high = high_ref[tile]
+        low = bounds_ref[0, tile]
+        high = bounds_ref[1, tile]
         there = pl.multiple_of(tile * TILE, TILE)
 
         @pl.when(high < low)
@@ -572,7 +652,7 @@
 
     def live_tile(tile, low, high, there):
         begin = begin_ref[pl.ds(tile, 1), :]
-        last = u_ref[pl.ds(tile, 1), :]
+        span = jnp.maximum(last_ref[pl.ds(tile, 1), :] - begin + 1, 0).astype(jnp.uint32)
         peak[...] = jnp.full_like(peak, NEG)
         summed[...] = jnp.zeros_like(summed)
         total[...] = jnp.zeros_like(total)
@@ -585,8 +665,7 @@
 
         def score_of(block, scores):
             holder, row = spot(block)
-            place = across + block * BLOCK
-            allowed = (place >= begin) & (place <= last)
+            allowed = (across + (block * BLOCK - begin)).astype(jnp.uint32) < span
             for head in range(2):
                 key = kv_ref[
                     holder,
@@ -647,23 +726,27 @@
                     one * TILE : (one + 1) * TILE
                 ]
 
-    lax.fori_loop(0, ROWS // TILE, one_tile, 0)
-
-
-def per_tile(column):
-    return jnp.tile(column.reshape(ROWS // TILE, TILE), (1, 8))
-
-
-def attend(low, high, u, begin, q, kv):
+    for sup in range(ROWS // SUPER):
+        load(sup).wait()
+        lax.fori_loop(sup * group, (sup + 1) * group, one_tile, 0)
+        store(sup).start()
+    for sup in range(ROWS // SUPER):
+        store(sup).wait()
+
+
+def attend(bounds, last, begin, q, kv):
     smem = pl.BlockSpec(memory_space=pltpu.SMEM)
     vmem = pl.BlockSpec(memory_space=pltpu.VMEM)
+    hbm = pl.BlockSpec(memory_space=pl.ANY)
     lanes = TILE * 8
     return pl.pallas_call(
         attend_kernel,
         out_shape=jax.ShapeDtypeStruct((ROWS, HALF), jnp.bfloat16),
-        in_specs=[smem] * 2 + [vmem] * 4,
-        out_specs=vmem,
+        in_specs=[smem, vmem, vmem, hbm, vmem],
+        out_specs=hbm,
         scratch_shapes=[
+            pltpu.VMEM((2, ROWS // TILE, lanes, HEAD_SIZE), jnp.bfloat16),
+            pltpu.VMEM((ROWS, HALF), jnp.bfloat16),
             pltpu.VMEM((2, 1, lanes), jnp.float32),
             pltpu.VMEM((2, HEAD_SIZE, lanes), jnp.float32),
             pltpu.VMEM((2, 1, lanes), jnp.float32),
@@ -672,22 +755,22 @@
             pltpu.VMEM((2, BLOCK, lanes), jnp.float32),
             pltpu.VMEM((2, BLOCK, lanes), jnp.bfloat16),
             pltpu.VMEM((2, BLOCK, lanes), jnp.bfloat16),
+            pltpu.SemaphoreType.DMA((ROWS // SUPER,)),
+            pltpu.SemaphoreType.DMA((ROWS // SUPER,)),
         ],
         compiler_params=pltpu.CompilerParams(vmem_limit_bytes=VMEM_LIMIT),
         name="attend",
-    )(low, high, per_tile(u), per_tile(begin), q, kv)
+    )(bounds, last, begin, q, kv)
 
 
 def local(queries, keys, values, plan, doc_lengths):
-    plan_col, plan_row = plan[:, None], plan[None, :]
-    lengths = jnp.pad(doc_lengths, ((0, 7), (0, 124)))
-    q, kv, places, rank = exchange(queries, keys, values, plan_col, plan_row, lengths)
-    u, begin = places[0], places[1]
-    live = u < 4096
-    low = jnp.where(live, begin // BLOCK, 0).reshape(ROWS // TILE, TILE)[:, 0]
-    high = jnp.max(jnp.where(live, u // BLOCK, -1).reshape(ROWS // TILE, TILE), 1)
-    made = attend(low, high, u, begin, q, kv)
-    return back(made, rank, plan_col, plan_row)
+    x, y, z, _ = coords()
+    my_cycle = x % 2 * 4 + y % 2 * 2 + z % 2
+    plan_row = plan[None, :]
+    q, kv, last, begin, bounds, rank = exchange(queries, keys, values, plan_row, doc_lengths)
+    made = attend(bounds, last, begin, q, kv)
+    ret = back(made, rank)
+    return restore(jnp.reshape(my_cycle, (1,)).astype(jnp.int32), plan_row, ret)
 
 
 def solution(mesh):

time: 185 us -> 172 us (0.930)
  local copies, waits for them, and re-layouts: 8.42 us -> 0 us
  Pallas kernels: 175 us -> 171 us
    pallas_call x1 -> x2, Pallas kernels: 61.1 us -> 47.7 us  [the longest x1 42.4 us: back(): pl.pallas_call(back_kernel, out_shape=jax.ShapeDtypeStruct((8, SLOT, 2 *...]
    pallas_call x1, Pallas kernels: 84.3 us -> 94.6 us  [exchange(): pl.pallas_call(exchange_kernel, out_shape=(jax.ShapeDtypeStruct((2, ROWS...]
    unnamed x1 -> x0, local copies, waits for them, and re-layouts: 3.13 us -> none
where the time goes in v3:
time: 172 us; the launch traced here: 171 us
  Pallas kernels  171 us (99%)
    pallas_call x1, Pallas kernels, exchange(): pl.pallas_call(exchange_kernel, out_shape=(jax.ShapeDtypeStruct((2, ROWS...  94.6 us
    pallas_call x1, Pallas kernels, back(): pl.pallas_call(back_kernel, out_shape=jax.ShapeDtypeStruct((8, SLOT, 2 *...  42.4 us
    pallas_call x1, Pallas kernels, attend(): pl.pallas_call(attend_kernel, out_shape=jax.ShapeDtypeStruct((ROWS, HALF)...  28.7 us
    pallas_call x1, Pallas kernels, restore(): pl.pallas_call(restore_kernel, grid=(2 * HALF // width,), out_shape=jax.S...  5.29 us

profile of v3, /device:TPU:1, one launch (start us, length us, event | category | flops | bytes accessed | tf_op | source)
XLA Modules:
  0.0 171.0 jit_solution(5023761810086581225)
XLA Ops:
  0.0 94.6 %exchange.1 = (bf16[2,32,256,128]{3,2,1,0:T(8,128)(2,1)}, bf16[8,512,512]{2,1,0:T(8,128)(2,1)}, s32[32,256]{1,0:T(8,128)}, s32[32,256]{1,0:T(8,128)}, s32[8,128]{1,0:T(8,128)}, /*index=5*/s32[1024,128]{1,0:T(8,128)}) custom-call(bf16[256,4096]{1,0:T(8,128)(2,1)} %queries_ref.1, bf16[256,512]{1,0:T(8,128)(2,1)} %keys_ref.1, bf16[256,512]{1,0:T(8,128)(2,1)} %values_ref.1, ...), custom_call_target="tpu_custom_call" | custom-call | tf_op jit(solution)/shard_map/exchange/pallas_call | solution.py:461
  94.6 28.7 %attend.1.made_ref = bf16[1024,2048]{1,0:T(8,128)(2,1)} custom-call(s32[8,128]{1,0:T(8,128)} %get-tuple-element.11.bounds_ref, s32[32,256]{1,0:T(8,128)} %get-tuple-element.12.last_ref, s32[32,256]{1,0:T(8,128)} %get-tuple-element.13.begin_ref, bf16[2,32,256,128]{3,2,1,0:T(8,128)(2,1)} %get-tuple-element.14.turned_ref, ...), custom_call_target="tpu_custom_call" | custom-call | tf_op jit(solution)/shard_map/attend/pallas_call | solution.py:742
  123.3 42.4 %back.1.ret_ref = bf16[8,64,4096]{2,1,0:T(8,128)(2,1)} custom-call(bf16[1024,2048]{1,0:T(8,128)(2,1)} %attend.1.made_ref, s32[1024,128]{1,0:T(8,128)} %get-tuple-element.16.rank_ref), custom_call_target="tpu_custom_call" | custom-call | tf_op jit(solution)/shard_map/back/pallas_call | solution.py:570
  165.7 5.3 %restore.1 = bf16[256,4096]{1,0:T(8,128)(2,1)} custom-call(s32[1]{0:T(128)} %bitcast.cycle_ref, s32[1,256]{1,0:T(1,128)} %bitcast.3, bf16[8,64,4096]{2,1,0:T(8,128)(2,1)} %back.1.ret_ref), custom_call_target="tpu_custom_call" | custom-call | tf_op jit(solution)/shard_map/restore/pallas_call | solution.py:604

commit v4 on v3

--- a/solution.py
+++ b/solution.py
@@ -16,7 +16,8 @@
 SLOT = 64
 KEYS = 512
 BLOCK = 256
-TILE = 32
+TILE = 64
+TILE_BITS = 6
 SUPER = 256
 HALF = QUERY_HEADS // 2 * HEAD_SIZE
 WIDE = HALF + 128
@@ -319,7 +320,7 @@
     lengths = len_got[...]
     begin_r = jnp.where(sorted_r < 4096, document_start(sorted_r, lengths), 8192)
 
-    own_tile = iota((ROWS // TILE, ROWS), 1) >> 5 == iota((ROWS // TILE, ROWS), 0)
+    own_tile = iota((ROWS // TILE, ROWS), 1) >> TILE_BITS == iota((ROWS // TILE, ROWS), 0)
     spread = bf16(iota((ROWS, TILE * 8), 0) & (TILE - 1) == iota((ROWS, TILE * 8), 1) & (TILE - 1))
     for values, tiles_ref in ((sorted_r, last_ref), (begin_r, begin_ref)):
         parts = [
@@ -338,7 +339,7 @@
         index, tile = iota((128, 128), 0) + base, iota((128, 128), 1)
         low = low + jnp.sum(jnp.where((index == tile * TILE) & live, start >> 8, 0), 0, keepdims=True)
         high = jnp.maximum(
-            high, jnp.max(jnp.where((index >> 5 == tile) & live, u >> 8, -1), 0, keepdims=True)
+            high, jnp.max(jnp.where((index >> TILE_BITS == tile) & live, u >> 8, -1), 0, keepdims=True)
         )
         cos, sin = turning(jnp.where(live, u - start, 0))
         cos_ref[pl.ds(base, 128), :] = cos * SCALE
@@ -618,78 +619,92 @@
 
 
 def attend_kernel(
-    bounds_ref, last_ref, begin_ref, turned_ref, kv_ref,
-    made_ref, turned, made, peak, total, summed, decays, scores0, scores1, weights0, weights1, in_sem, out_sem,
+    bounds_ref, last_ref, begin_ref, turned_ref, all_ref,
+    made_ref, turned, kv_ref, made, peak, total, summed, decays, scores0, scores1, weights0, weights1, items, in_sem, out_sem,
 ):
     across = iota((BLOCK, TILE * 8), 0)
-    group = SUPER // TILE
-
-    def load(sup):
-        tiles = pl.ds(sup * group, group)
-        return pltpu.make_async_copy(turned_ref.at[:, tiles], turned.at[:, tiles], in_sem.at[sup])
-
-    def store(sup):
-        rows = pl.ds(sup * SUPER, SUPER)
-        return pltpu.make_async_copy(made.at[rows], made_ref.at[rows], out_sem.at[sup])
-
-    for sup in range(ROWS // SUPER):
-        load(sup).start()
-
-    def one_tile(tile, carry):
+    tiles = ROWS // TILE
+    loads = (
+        pltpu.make_async_copy(turned_ref, turned, in_sem.at[0]),
+        pltpu.make_async_copy(all_ref, kv_ref, in_sem.at[1]),
+    )
+    for load in loads:
+        load.start()
+
+    def store(tile):
+        rows = pl.ds(pl.multiple_of(tile * TILE, TILE), TILE)
+        return pltpu.make_async_copy(made.at[rows], made_ref.at[rows], out_sem)
+
+    def list_tile(tile, count):
         low = bounds_ref[0, tile]
         high = bounds_ref[1, tile]
-        there = pl.multiple_of(tile * TILE, TILE)
+
+        def list_block(block, count):
+            items[0, count] = tile
+            items[1, count] = block
+            items[2, count] = (block == low).astype(jnp.int32)
+            items[3, count] = (block == high).astype(jnp.int32)
+            return count + 1
 
         @pl.when(high < low)
         def _():
-            made[pl.ds(there, TILE), :] = jnp.zeros((TILE, HALF), jnp.bfloat16)
-
-        @pl.when(high >= low)
-        def _():
-            live_tile(tile, low, high, there)
-
-        return carry
-
-    def live_tile(tile, low, high, there):
+            made[pl.ds(pl.multiple_of(tile * TILE, TILE), TILE), :] = jnp.zeros((TILE, HALF), jnp.bfloat16)
+            store(tile).start()
+
+        return lax.fori_loop(low, high + 1, list_block, count)
+
+    count = lax.fori_loop(0, tiles, list_tile, 0)
+    for extra in range(3):
+        items[0, count + extra] = items[0, count - 1]
+        items[1, count + extra] = 32
+        items[2, count + extra] = 0
+        items[3, count + extra] = 0
+
+    peak[...] = jnp.full_like(peak, NEG)
+    summed[...] = jnp.zeros_like(summed)
+    total[...] = jnp.zeros_like(total)
+    decays[...] = jnp.ones_like(decays)
+    weights1[...] = jnp.zeros_like(weights1)
+    for load in loads:
+        load.wait()
+
+    def spot(block):
+        block = jnp.minimum(block, 15)
+        return jnp.where(block < 8, block, 15 - block), jnp.where(block < 8, 0, BLOCK)
+
+    def score_of(item, scores):
+        tile, block = items[0, item], items[1, item]
         begin = begin_ref[pl.ds(tile, 1), :]
         span = jnp.maximum(last_ref[pl.ds(tile, 1), :] - begin + 1, 0).astype(jnp.uint32)
-        peak[...] = jnp.full_like(peak, NEG)
-        summed[...] = jnp.zeros_like(summed)
-        total[...] = jnp.zeros_like(total)
-        decays[...] = jnp.ones_like(decays)
-        weights1[...] = jnp.zeros_like(weights1)
-
-        def spot(block):
-            block = jnp.minimum(block, 15)
-            return jnp.where(block < 8, block, 15 - block), jnp.where(block < 8, 0, BLOCK)
-
-        def score_of(block, scores):
-            holder, row = spot(block)
-            allowed = (across + (block * BLOCK - begin)).astype(jnp.uint32) < span
-            for head in range(2):
-                key = kv_ref[
-                    holder,
-                    pl.ds(pl.multiple_of(row, BLOCK), BLOCK),
-                    head * HEAD_SIZE : (head + 1) * HEAD_SIZE,
-                ]
-                score = lax.dot_general(
-                    key, turned[head, tile], (((1,), (1,)), ((), ())), preferred_element_type=jnp.float32
-                )
-                scores[head] = jnp.where(allowed, score, NEG)
-
-        def weigh(scores, weights, head):
+        holder, row = spot(block)
+        allowed = (across + (block * BLOCK - begin)).astype(jnp.uint32) < span
+        for head in range(2):
+            key = kv_ref[
+                holder,
+                pl.ds(pl.multiple_of(row, BLOCK), BLOCK),
+                head * HEAD_SIZE : (head + 1) * HEAD_SIZE,
+            ]
+            score = lax.dot_general(
+                key, turned[head, tile], (((1,), (1,)), ((), ())), preferred_element_type=jnp.float32
+            )
+            scores[head] = jnp.where(allowed, score, NEG)
+
+    def weigh(item, scores, weights):
+        opens = items[2, item] == 1
+        for head in range(2):
             score = scores[head]
-            old = peak[head]
+            old = jnp.where(opens, NEG, peak[head])
             new = jnp.maximum(old, jnp.max(score, 0, keepdims=True))
-            decay = jnp.exp2(old - new)
+            decay = jnp.where(opens, 0.0, jnp.exp2(old - new))
             peak[head] = new
             weight = jnp.exp2(score - new)
             summed[head] = summed[head] * decay + jnp.sum(weight, 0, keepdims=True)
             weights[head] = weight.astype(jnp.bfloat16)
             decays[head] = decay
 
-        def add(block, weights, head):
-            holder, row = spot(block)
+    def add(item, weights):
+        holder, row = spot(items[1, item])
+        for head in range(2):
             value = kv_ref[
                 holder,
                 pl.ds(pl.multiple_of(row + head * HEAD_SIZE, HEAD_SIZE), HEAD_SIZE),
@@ -699,39 +714,38 @@
                 value, weights[head], preferred_element_type=jnp.float32
             )
 
-        score_of(low, scores0)
-
-        def one_step(step, carry):
-            block = low + step * 2
+    score_of(0, scores0)
+
+    def two_steps(pair, carry):
+        item = pair * 2
+        add(jnp.maximum(item - 1, 0), weights1)
+        score_of(item + 1, scores1)
+        keep = summed[...]
+        weigh(item, scores0, weights0)
+        close_after(item - 1, keep)
+        add(item, weights0)
+        score_of(item + 2, scores0)
+        keep = summed[...]
+        weigh(item + 1, scores1, weights1)
+        close_after(item, keep)
+        return carry
+
+    def close_after(item, sums):
+        at = jnp.maximum(item, 0)
+
+        @pl.when((items[3, at] == 1) & (item >= 0))
+        def _():
+            there = pl.multiple_of(items[0, at] * TILE, TILE)
             for head in range(2):
-                add(jnp.maximum(block - 1, 0), weights1, head)
-            score_of(block + 1, scores1)
-            for head in range(2):
-                weigh(scores0, weights0, head)
-            for head in range(2):
-                add(block, weights0, head)
-            score_of(block + 2, scores0)
-            for head in range(2):
-                weigh(scores1, weights1, head)
-            return carry
-
-        steps = (high - low + 2) // 2
-        lax.fori_loop(0, steps, one_step, 0)
-        for head in range(2):
-            add(jnp.maximum(low + steps * 2 - 1, 0), weights1, head)
-        for head in range(2):
-            result = (total[head] / jnp.maximum(summed[head], 1e-30)).T.astype(jnp.bfloat16)
-            for one in range(8):
-                made[pl.ds(there, TILE), pl.ds((head * 8 + one) * HEAD_SIZE, HEAD_SIZE)] = result[
-                    one * TILE : (one + 1) * TILE
-                ]
-
-    for sup in range(ROWS // SUPER):
-        load(sup).wait()
-        lax.fori_loop(sup * group, (sup + 1) * group, one_tile, 0)
-        store(sup).start()
-    for sup in range(ROWS // SUPER):
-        store(sup).wait()
+                result = (total[head] / jnp.maximum(sums[head], 1e-30)).T.astype(jnp.bfloat16)
+                for one in range(8):
+                    made[pl.ds(there, TILE), pl.ds((head * 8 + one) * HEAD_SIZE, HEAD_SIZE)] = result[
+                        one * TILE : (one + 1) * TILE
+                    ]
+            store(items[0, at]).start()
+
+    lax.fori_loop(0, (count + 2) // 2, two_steps, 0)
+    pltpu.make_async_copy(made, made_ref, out_sem).wait()
 
 
 def attend(bounds, last, begin, q, kv):
@@ -742,10 +756,11 @@
     return pl.pallas_call(
         attend_kernel,
         out_shape=jax.ShapeDtypeStruct((ROWS, HALF), jnp.bfloat16),
-        in_specs=[smem, vmem, vmem, hbm, vmem],
+        in_specs=[smem, vmem, vmem, hbm, hbm],
         out_specs=hbm,
         scratch_shapes=[
             pltpu.VMEM((2, ROWS // TILE, lanes, HEAD_SIZE), jnp.bfloat16),
+            pltpu.VMEM((8, KEYS, 512), jnp.bfloat16),
             pltpu.VMEM((ROWS, HALF), jnp.bfloat16),
             pltpu.VMEM((2, 1, lanes), jnp.float32),
             pltpu.VMEM((2, HEAD_SIZE, lanes), jnp.float32),
@@ -755,8 +770,9 @@
             pltpu.VMEM((2, BLOCK, lanes), jnp.float32),
             pltpu.VMEM((2, BLOCK, lanes), jnp.bfloat16),
             pltpu.VMEM((2, BLOCK, lanes), jnp.bfloat16),
-            pltpu.SemaphoreType.DMA((ROWS // SUPER,)),
-            pltpu.SemaphoreType.DMA((ROWS // SUPER,)),
+            pltpu.SMEM((4, ROWS // TILE * 16 + 4), jnp.int32),
+            pltpu.SemaphoreType.DMA((2,)),
+            pltpu.SemaphoreType.DMA(()),
         ],
         compiler_params=pltpu.CompilerParams(vmem_limit_bytes=VMEM_LIMIT),
         name="attend",

time: 172 us -> 169 us (0.983)
  Pallas kernels: 171 us -> 168 us
    pallas_call x1, Pallas kernels: 28.7 us -> 24.7 us  [attend(): pl.pallas_call(attend_kernel, out_shape=jax.ShapeDtypeStruct((ROWS, HALF)...]
where the time goes in v4:
time: 169 us; the launch traced here: 168 us
  Pallas kernels  168 us (99%)
    pallas_call x1, Pallas kernels, exchange(): pl.pallas_call(exchange_kernel, out_shape=(jax.ShapeDtypeStruct((2, ROWS...  94.6 us
    pallas_call x1, Pallas kernels, back(): pl.pallas_call(back_kernel, out_shape=jax.ShapeDtypeStruct((8, SLOT, 2 *...  43.7 us
    pallas_call x1, Pallas kernels, attend(): pl.pallas_call(attend_kernel, out_shape=jax.ShapeDtypeStruct((ROWS, HALF)...  24.7 us
    pallas_call x1, Pallas kernels, restore(): pl.pallas_call(restore_kernel, grid=(2 * HALF // width,), out_shape=jax.S...  5.29 us

profile of v4, /device:TPU:1, one launch (start us, length us, event | category | flops | bytes accessed | tf_op | source)
XLA Modules:
  0.0 168.3 jit_solution(10175926240669202067)
XLA Ops:
  0.0 94.6 %exchange.1 = (bf16[2,16,512,128]{3,2,1,0:T(8,128)(2,1)}, bf16[8,512,512]{2,1,0:T(8,128)(2,1)}, s32[16,512]{1,0:T(8,128)}, s32[16,512]{1,0:T(8,128)}, s32[8,128]{1,0:T(8,128)}, /*index=5*/s32[1024,128]{1,0:T(8,128)}) custom-call(bf16[256,4096]{1,0:T(8,128)(2,1)} %queries_ref.1, bf16[256,512]{1,0:T(8,128)(2,1)} %keys_ref.1, bf16[256,512]{1,0:T(8,128)(2,1)} %values_ref.1, ...), custom_call_target="tpu_custom_call" | custom-call | tf_op jit(solution)/shard_map/exchange/pallas_call | solution.py:462
  94.6 24.7 %attend.1.made_ref = bf16[1024,2048]{1,0:T(8,128)(2,1)} custom-call(s32[8,128]{1,0:T(8,128)} %get-tuple-element.11.bounds_ref, s32[16,512]{1,0:T(8,128)} %get-tuple-element.12.last_ref, s32[16,512]{1,0:T(8,128)} %get-tuple-element.13.begin_ref, bf16[2,16,512,128]{3,2,1,0:T(8,128)(2,1)} %get-tuple-element.14.turned_ref, ...), custom_call_target="tpu_custom_call" | custom-call | tf_op jit(solution)/shard_map/attend/pallas_call | solution.py:756
  119.4 43.7 %back.1.ret_ref = bf16[8,64,4096]{2,1,0:T(8,128)(2,1)} custom-call(bf16[1024,2048]{1,0:T(8,128)(2,1)} %attend.1.made_ref, s32[1024,128]{1,0:T(8,128)} %get-tuple-element.16.rank_ref), custom_call_target="tpu_custom_call" | custom-call | tf_op jit(solution)/shard_map/back/pallas_call | solution.py:571
  163.0 5.3 %restore.1 = bf16[256,4096]{1,0:T(8,128)(2,1)} custom-call(s32[1]{0:T(128)} %bitcast.cycle_ref, s32[1,256]{1,0:T(1,128)} %bitcast.3, bf16[8,64,4096]{2,1,0:T(8,128)(2,1)} %back.1.ret_ref), custom_call_target="tpu_custom_call" | custom-call | tf_op jit(solution)/shard_map/restore/pallas_call | solution.py:605

commit v5 on v4

--- a/solution.py
+++ b/solution.py
@@ -59,7 +59,7 @@
 
 
 THIRDS = ((0, 176, (4, 2, 1)), (176, 176, (2, 1, 4)), (352, 160, (1, 4, 2)))
-PAIR = 640
+PAIR = 512
 PART = 128
 
 
@@ -115,8 +115,9 @@
 def exchange_kernel(
     queries_ref, keys_ref, values_ref, plan_row, lengths_ref,
     turned_ref, all_ref, last_ref, begin_ref, bounds_ref, rank_ref,
-    q_out, q_got, kv_out, kv_got, part_out, part_got, own_ref, len_out, len_got, key_ref, cos_ref, sin_ref, sorted_ref,
+    q_out, q_got, kv_out, kv_got, part_out, part_got, f_out, f_got, g_out, g_got, own_ref, len_out, len_got, key_ref, cos_ref, sin_ref, sorted_ref,
     q_send, q_recv, a_send, a_recv, b_send, b_recv, kv_send, kv_recv, len_send, len_recv, local_sem, out_sem,
+    f_send, f_recv, g_send, g_recv,
 ):
     x, y, z, core = coords()
     place = x // 2 * 4 + y // 2 * 2 + z // 2
@@ -155,15 +156,7 @@
     lane = iota((TOK, 128), 1)
     fields = jnp.where(lane == 0, (u >> 8) + 1, jnp.where(lane == 1, u & 255, 0))
     fields = fields.astype(jnp.float32).astype(jnp.bfloat16)
-    chosen_k = dot(choose, keys_ref[...]).astype(jnp.bfloat16)
-    chosen_v = dot(choose, values_ref[...]).astype(jnp.bfloat16)
-    chosen_f = dot(choose, fields).astype(jnp.bfloat16)
-    for delta in range(8):
-        rows = slice(delta * SLOT, (delta + 1) * SLOT)
-        for half in range(2):
-            kv_out[delta, :, half * PAIR : half * PAIR + 256] = chosen_k[rows, half * 256 : half * 256 + 256]
-            kv_out[delta, :, half * PAIR + 256 : half * PAIR + 512] = chosen_v[rows, half * 256 : half * 256 + 256]
-            kv_out[delta, :, half * PAIR + 512 : half * PAIR + 640] = chosen_f[rows, :]
+    f_out[...] = dot(choose, fields).astype(jnp.bfloat16).reshape(8, SLOT, 128)
 
     pl.semaphore_wait(pltpu.get_barrier_semaphore(), jnp.where(at_home, 22, 23))
 
@@ -196,6 +189,29 @@
         remote(here, here, send.at[0], recv.at[delta, source], moved(0, 0, other)).wait_recv()
 
     order = (7, 6, 5, 3, 4, 2, 1)
+
+    def f_copy(delta, to_core):
+        return remote(
+            f_out.at[delta],
+            f_got.at[delta, core],
+            f_send.at[delta * 2 + to_core if delta else 0],
+            f_recv.at[delta, core],
+            moved(mine, delta, to_core),
+        )
+
+    start(f_copy(0, other))
+    for delta in order:
+        for to_core in range(2):
+            start(f_copy(delta, to_core))
+    f_got[0, core] = f_out[0]
+
+    chosen_k = dot(choose, keys_ref[...]).astype(jnp.bfloat16)
+    chosen_v = dot(choose, values_ref[...]).astype(jnp.bfloat16)
+    for delta in range(8):
+        rows = slice(delta * SLOT, (delta + 1) * SLOT)
+        for half in range(2):
+            kv_out[delta, :, half * PAIR : half * PAIR + 256] = chosen_k[rows, half * 256 : half * 256 + 256]
+            kv_out[delta, :, half * PAIR + 256 : half * PAIR + 512] = chosen_v[rows, half * 256 : half * 256 + 256]
     start(out_copy(kv_out, kv_got, a_send, a_recv, PAIR, 0, other))
     for delta in order:
         for to_core in range(2):
@@ -211,7 +227,7 @@
         for delta in range(8):
             q_out[delta, :, columns] = chosen[delta * SLOT : (delta + 1) * SLOT, :]
     start(out_copy(q_out, q_got, q_send, q_recv, HALF, 0, other))
-    for chunk in range(SLOT // 16):
+    def send_queries(chunk):
         for delta in order:
             for to_core in range(2):
                 columns = pl.ds(to_core * HALF, HALF)
@@ -223,6 +239,8 @@
                     q_recv.at[delta, core],
                     moved(mine, delta, to_core),
                 ).start()
+
+    send_queries(0)
     for delta in order:
         for to_core in range(2):
             copies.append(out_copy(q_out, q_got, q_send, q_recv, HALF, delta, to_core))
@@ -231,11 +249,10 @@
     )
     own_q.start()
 
-    own_a.wait()
-    landed(kv_got, a_send, a_recv, 0, other)
+    landed(f_got, f_send, f_recv, 0, other)
     for delta in range(1, 8):
         for source in range(2):
-            landed(kv_got, a_send, a_recv, delta, source)
+            landed(f_got, f_send, f_recv, delta, source)
 
     def fields_of(table):
         fields = table.reshape(ROWS, 128).astype(jnp.float32)
@@ -250,7 +267,7 @@
         block = u >> 8
         return jnp.where(block < 8, block, 15 - block)
 
-    (valid_c, u_c), (valid_r, u_r) = fields_of(kv_got[:, :, :, 512:])
+    (valid_c, u_c), (valid_r, u_r) = fields_of(f_got[...])
     key_c = jnp.where(valid_c, holder_of(u_c), -1)
     key_r = jnp.where(valid_r, holder_of(u_r), -2)
     key_ref[...] = jnp.broadcast_to(key_c, (ROWS, 128))
@@ -263,14 +280,6 @@
 
     before = lax.fori_loop(0, ROWS // 128, count_before, jnp.zeros((1, ROWS), jnp.int32))
     target = jnp.where(valid_r, key_r * PART + before, -1)
-
-    def fill(step, carry):
-        base = pl.multiple_of(step * 4 * PART, 4 * PART)
-        rows = dot(bf16(iota((4 * PART, ROWS), 0) + base == target), kv_got[...].reshape(ROWS, PAIR))
-        part_out[pl.ds(step * 4, 4)] = rows.astype(jnp.bfloat16).reshape(4, PART, PAIR)
-        return carry
-
-    lax.fori_loop(0, 2, fill, 0)
 
     def flip(mask):
         out = 0
@@ -279,12 +288,39 @@
             out = out + bit * ((1 - digit) if mask & bit else digit)
         return out
 
+    def place_fields(step, carry):
+        base = pl.multiple_of(step * 4 * PART, 4 * PART)
+        rows = dot(bf16(iota((4 * PART, ROWS), 0) + base == target), f_got[...].reshape(ROWS, 128))
+        g_out[pl.ds(step * 4, 4)] = rows.astype(jnp.bfloat16).reshape(4, PART, 128)
+        return carry
+
+    lax.fori_loop(0, 2, place_fields, 0)
+    for mask in order:
+        start(remote(g_out.at[flip(mask)], g_got.at[place], g_send.at[mask], g_recv.at[mask], across_cycle(mask)))
+    send_queries(1)
+    g_got[place] = g_out[place]
+
+    own_a.wait()
+    landed(kv_got, a_send, a_recv, 0, other)
+    for delta in range(1, 8):
+        for source in range(2):
+            landed(kv_got, a_send, a_recv, delta, source)
+
+    def fill(step, carry):
+        base = pl.multiple_of(step * 4 * PART, 4 * PART)
+        rows = dot(bf16(iota((4 * PART, ROWS), 0) + base == target), kv_got[...].reshape(ROWS, PAIR))
+        part_out[pl.ds(step * 4, 4)] = rows.astype(jnp.bfloat16).reshape(4, PART, PAIR)
+        return carry
+
+    lax.fori_loop(0, 2, fill, 0)
+
     for mask in order:
         start(
             remote(
                 part_out.at[flip(mask)], part_got.at[place], b_send.at[mask], b_recv.at[mask], across_cycle(mask)
             )
         )
+    send_queries(2)
     part_got[place] = part_out[place]
 
     index_c, index_r = iota((ROWS, 1), 0), iota((1, ROWS), 1)
@@ -357,12 +393,17 @@
     key_cos, key_sin = turning(key_u - document_start(key_u, lengths))
 
     for mask in range(1, 8):
+        here = g_got.at[flip(mask)]
+        remote(here, here, g_send.at[mask], g_recv.at[mask], across_cycle(mask)).wait_recv()
+    _, (valid, u) = fields_of(g_got[...])
+    target = jnp.where(valid, jnp.where(u >= 2048, BLOCK, 0) + (u & 255), -1)
+    arrange = bf16(iota((KEYS, ROWS), 0) == target)
+
+    for mask in range(1, 8):
         here = part_got.at[flip(mask)]
         remote(here, here, b_send.at[mask], b_recv.at[mask], across_cycle(mask)).wait_recv()
 
-    _, (valid, u) = fields_of(part_got[:, :, 512:])
-    target = jnp.where(valid, jnp.where(u >= 2048, BLOCK, 0) + (u & 255), -1)
-    placed = dot(bf16(iota((KEYS, ROWS), 0) == target), part_got[:, :, :512].reshape(ROWS, 512))
+    placed = dot(arrange, part_got[...].reshape(ROWS, PAIR))
     for head in range(2):
         columns = slice(head * HEAD_SIZE, (head + 1) * HEAD_SIZE)
         entry = placed[:, columns]
@@ -395,6 +436,7 @@
         for third in range(3):
             start(kv_copy(third, index))
 
+    send_queries(3)
     landed(q_got, q_send, q_recv, 0, other)
     for delta in range(1, 8):
         for source in range(2):
@@ -478,6 +520,10 @@
             pltpu.VMEM((8, 2, SLOT, PAIR), jnp.bfloat16),
             pltpu.VMEM((8, PART, PAIR), jnp.bfloat16),
             pltpu.VMEM((8, PART, PAIR), jnp.bfloat16),
+            pltpu.VMEM((8, SLOT, 128), jnp.bfloat16),
+            pltpu.VMEM((8, 2, SLOT, 128), jnp.bfloat16),
+            pltpu.VMEM((8, PART, 128), jnp.bfloat16),
+            pltpu.VMEM((8, PART, 128), jnp.bfloat16),
             pltpu.VMEM((KEYS, 512), jnp.bfloat16),
             pltpu.VMEM((8, 128), jnp.int32),
             pltpu.VMEM((8, 128), jnp.int32),
@@ -486,7 +532,7 @@
             pltpu.VMEM((ROWS, HEAD_SIZE), jnp.float32),
             pltpu.VMEM((2, ROWS // TILE, TILE * 8, HEAD_SIZE), jnp.bfloat16),
             dma((16,)), dma((8, 2)), dma((16,)), dma((8, 2)), dma((8,)), dma((8,)), dma((3, 7)), dma((3, 7)),
-            dma(()), dma(()), dma((3,)), dma((4,)),
+            dma(()), dma(()), dma((3,)), dma((4,)), dma((16,)), dma((8, 2)), dma((8,)), dma((8,)),
         ],
         compiler_params=pltpu.CompilerParams(
             collective_id=0, has_side_effects=True, vmem_limit_bytes=VMEM_LIMIT
@@ -601,7 +647,7 @@
 
 
 def restore(my_cycle, plan_row, ret):
-    width = 1024
+    width = 2048
     return pl.pallas_call(
         restore_kernel,
         grid=(2 * HALF // width,),

time: 169 us -> 163 us (0.964)
  Pallas kernels: 168 us -> 163 us
    pallas_call x1, Pallas kernels: 43.7 us -> 38.9 us  [back(): pl.pallas_call(back_kernel, out_shape=jax.ShapeDtypeStruct((8, SLOT, 2 *...]
where the time goes in v5:
time: 163 us
  Pallas kernels  163 us (100%)
    pallas_call x1, Pallas kernels, exchange(): pl.pallas_call(exchange_kernel, out_shape=(jax.ShapeDtypeStruct((2, ROWS...  93.5 us
    pallas_call x1, Pallas kernels, back(): pl.pallas_call(back_kernel, out_shape=jax.ShapeDtypeStruct((8, SLOT, 2 *...  38.9 us
    pallas_call x1, Pallas kernels, attend(): pl.pallas_call(attend_kernel, out_shape=jax.ShapeDtypeStruct((ROWS, HALF)...  26.2 us
    pallas_call x1, Pallas kernels, restore(): pl.pallas_call(restore_kernel, grid=(2 * HALF // width,), out_shape=jax.S...  4.3 us

profile of v5, /device:TPU:1, one launch (start us, length us, event | category | flops | bytes accessed | tf_op | source)
XLA Modules:
  0.0 162.9 jit_solution(14573658249717032307)
XLA Ops:
  0.0 93.5 %exchange.1 = (bf16[2,16,512,128]{3,2,1,0:T(8,128)(2,1)}, bf16[8,512,512]{2,1,0:T(8,128)(2,1)}, s32[16,512]{1,0:T(8,128)}, s32[16,512]{1,0:T(8,128)}, s32[8,128]{1,0:T(8,128)}, /*index=5*/s32[1024,128]{1,0:T(8,128)}) custom-call(bf16[256,4096]{1,0:T(8,128)(2,1)} %queries_ref.1, bf16[256,512]{1,0:T(8,128)(2,1)} %keys_ref.1, bf16[256,512]{1,0:T(8,128)(2,1)} %values_ref.1, ...), custom_call_target="tpu_custom_call" | custom-call | tf_op jit(solution)/shard_map/exchange/pallas_call | solution.py:504
  93.5 26.2 %attend.1.made_ref = bf16[1024,2048]{1,0:T(8,128)(2,1)} custom-call(s32[8,128]{1,0:T(8,128)} %get-tuple-element.11.bounds_ref, s32[16,512]{1,0:T(8,128)} %get-tuple-element.12.last_ref, s32[16,512]{1,0:T(8,128)} %get-tuple-element.13.begin_ref, bf16[2,16,512,128]{3,2,1,0:T(8,128)(2,1)} %get-tuple-element.14.turned_ref, ...), custom_call_target="tpu_custom_call" | custom-call | tf_op jit(solution)/shard_map/attend/pallas_call | solution.py:802
  119.7 38.9 %back.1.ret_ref = bf16[8,64,4096]{2,1,0:T(8,128)(2,1)} custom-call(bf16[1024,2048]{1,0:T(8,128)(2,1)} %attend.1.made_ref, s32[1024,128]{1,0:T(8,128)} %get-tuple-element.16.rank_ref), custom_call_target="tpu_custom_call" | custom-call | tf_op jit(solution)/shard_map/back/pallas_call | solution.py:617
  158.6 4.3 %restore.1 = bf16[256,4096]{1,0:T(8,128)(2,1)} custom-call(s32[1]{0:T(128)} %bitcast.cycle_ref, s32[1,256]{1,0:T(1,128)} %bitcast.3, bf16[8,64,4096]{2,1,0:T(8,128)(2,1)} %back.1.ret_ref), custom_call_target="tpu_custom_call" | custom-call | tf_op jit(solution)/shard_map/restore/pallas_call | solution.py:651

commit v6 on v5

--- a/solution.py
+++ b/solution.py
@@ -552,15 +552,15 @@
 
     columns = pl.ds(pl.multiple_of(core * HALF, 128), HALF)
 
-    def place_rows(first):
-        rows = slice(first * 2 * SLOT, first * 2 * SLOT + 4 * SLOT)
-        put = bf16(rank_ref[rows, 0:1] == iota((4 * SLOT, ROWS), 1))
+    def place_rows(pair):
+        ranks = [rank_ref[delta * 2 * SLOT : (delta + 1) * 2 * SLOT, 0:1] for delta in pair]
+        put = bf16(jnp.concatenate(ranks, 0) == iota((4 * SLOT, ROWS), 1))
 
         def one_part(part, carry):
             here = pl.ds(pl.multiple_of(part * 512, 512), 512)
             chosen = dot(put, made_ref[:, here]).astype(jnp.bfloat16)
             for one in range(4):
-                send_ref[first + one // 2, one % 2, :, here] = chosen[one * SLOT : (one + 1) * SLOT, :]
+                send_ref[pair[one // 2], one % 2, :, here] = chosen[one * SLOT : (one + 1) * SLOT, :]
             return carry
 
         lax.fori_loop(0, 4, one_part, 0)
@@ -577,12 +577,13 @@
             moved(-sign_of(source), delta, source),
         )
 
-    place_rows(6)
+    pairs = ((7, 0), (6, 1), (5, 2), (3, 4))
+    place_rows(pairs[0])
     pl.semaphore_wait(pltpu.get_barrier_semaphore(), 15)
-    for first in (6, 4, 2, 0):
-        if first < 6:
-            place_rows(first)
-        deltas = [delta for delta in (first + 1, first) if delta]
+    for pair in pairs:
+        if pair != pairs[0]:
+            place_rows(pair)
+        deltas = [delta for delta in pair if delta]
         for chunk in range(SLOT // 16):
             for delta in deltas:
                 for source in range(2):

time: 163 us -> 160 us (0.982)
  Pallas kernels: 163 us -> 160 us
    pallas_call x1, Pallas kernels: 38.9 us -> 33.5 us  [back(): pl.pallas_call(back_kernel, out_shape=jax.ShapeDtypeStruct((8, SLOT, 2 *...]
    pallas_call x1, Pallas kernels: 26.2 us -> 28.6 us  [attend(): pl.pallas_call(attend_kernel, out_shape=jax.ShapeDtypeStruct((ROWS, HALF)...]
where the time goes in v6:
time: 160 us
  Pallas kernels  160 us (100%)
    pallas_call x1, Pallas kernels, exchange(): pl.pallas_call(exchange_kernel, out_shape=(jax.ShapeDtypeStruct((2, ROWS...  93.5 us
    pallas_call x1, Pallas kernels, back(): pl.pallas_call(back_kernel, out_shape=jax.ShapeDtypeStruct((8, SLOT, 2 *...  33.5 us
    pallas_call x1, Pallas kernels, attend(): pl.pallas_call(attend_kernel, out_shape=jax.ShapeDtypeStruct((ROWS, HALF)...  28.6 us
    pallas_call x1, Pallas kernels, restore(): pl.pallas_call(restore_kernel, grid=(2 * HALF // width,), out_shape=jax.S...  4.3 us

profile of v6, /device:TPU:1, one launch (start us, length us, event | category | flops | bytes accessed | tf_op | source)
XLA Modules:
  0.0 159.9 jit_solution(2933599452887222199)
XLA Ops:
  0.0 93.5 %exchange.1 = (bf16[2,16,512,128]{3,2,1,0:T(8,128)(2,1)}, bf16[8,512,512]{2,1,0:T(8,128)(2,1)}, s32[16,512]{1,0:T(8,128)}, s32[16,512]{1,0:T(8,128)}, s32[8,128]{1,0:T(8,128)}, /*index=5*/s32[1024,128]{1,0:T(8,128)}) custom-call(bf16[256,4096]{1,0:T(8,128)(2,1)} %queries_ref.1, bf16[256,512]{1,0:T(8,128)(2,1)} %keys_ref.1, bf16[256,512]{1,0:T(8,128)(2,1)} %values_ref.1, ...), custom_call_target="tpu_custom_call" | custom-call | tf_op jit(solution)/shard_map/exchange/pallas_call | solution.py:504
  93.5 28.6 %attend.1.made_ref = bf16[1024,2048]{1,0:T(8,128)(2,1)} custom-call(s32[8,128]{1,0:T(8,128)} %get-tuple-element.11.bounds_ref, s32[16,512]{1,0:T(8,128)} %get-tuple-element.12.last_ref, s32[16,512]{1,0:T(8,128)} %get-tuple-element.13.begin_ref, bf16[2,16,512,128]{3,2,1,0:T(8,128)(2,1)} %get-tuple-element.14.turned_ref, ...), custom_call_target="tpu_custom_call" | custom-call | tf_op jit(solution)/shard_map/attend/pallas_call | solution.py:803
  122.1 33.5 %back.1.ret_ref = bf16[8,64,4096]{2,1,0:T(8,128)(2,1)} custom-call(bf16[1024,2048]{1,0:T(8,128)(2,1)} %attend.1.made_ref, s32[1024,128]{1,0:T(8,128)} %get-tuple-element.16.rank_ref), custom_call_target="tpu_custom_call" | custom-call | tf_op jit(solution)/shard_map/back/pallas_call | solution.py:618
  155.6 4.3 %restore.1 = bf16[256,4096]{1,0:T(8,128)(2,1)} custom-call(s32[1]{0:T(128)} %bitcast.cycle_ref, s32[1,256]{1,0:T(1,128)} %bitcast.3, bf16[8,64,4096]{2,1,0:T(8,128)(2,1)} %back.1.ret_ref), custom_call_target="tpu_custom_call" | custom-call | tf_op jit(solution)/shard_map/restore/pallas_call | solution.py:652

commit v7 on v6

--- a/solution.py
+++ b/solution.py
@@ -702,7 +702,7 @@
 
     count = lax.fori_loop(0, tiles, list_tile, 0)
     for extra in range(3):
-        items[0, count + extra] = items[0, count - 1]
+        items[0, count + extra] = 0
         items[1, count + extra] = 32
         items[2, count + extra] = 0
         items[3, count + extra] = 0

time: 160 us -> 163 us (1.019)
  Pallas kernels: 160 us -> 162 us
where the time goes in v7:
time: 163 us; the launch traced here: 162 us
  Pallas kernels  162 us (99%)
    pallas_call x1, Pallas kernels, exchange(): pl.pallas_call(exchange_kernel, out_shape=(jax.ShapeDtypeStruct((2, ROWS...  93.5 us
    pallas_call x1, Pallas kernels, back(): pl.pallas_call(back_kernel, out_shape=jax.ShapeDtypeStruct((8, SLOT, 2 *...  34.5 us
    pallas_call x1, Pallas kernels, attend(): pl.pallas_call(attend_kernel, out_shape=jax.ShapeDtypeStruct((ROWS, HALF)...  30.1 us
    pallas_call x1, Pallas kernels, restore(): pl.pallas_call(restore_kernel, grid=(2 * HALF // width,), out_shape=jax.S...  4.31 us

profile of v7, /device:TPU:1, one launch (start us, length us, event | category | flops | bytes accessed | tf_op | source)
XLA Modules:
  0.0 162.4 jit_solution(12748912478720751349)
XLA Ops:
  0.0 93.5 %exchange.1 = (bf16[2,16,512,128]{3,2,1,0:T(8,128)(2,1)}, bf16[8,512,512]{2,1,0:T(8,128)(2,1)}, s32[16,512]{1,0:T(8,128)}, s32[16,512]{1,0:T(8,128)}, s32[8,128]{1,0:T(8,128)}, /*index=5*/s32[1024,128]{1,0:T(8,128)}) custom-call(bf16[256,4096]{1,0:T(8,128)(2,1)} %queries_ref.1, bf16[256,512]{1,0:T(8,128)(2,1)} %keys_ref.1, bf16[256,512]{1,0:T(8,128)(2,1)} %values_ref.1, ...), custom_call_target="tpu_custom_call" | custom-call | tf_op jit(solution)/shard_map/exchange/pallas_call | solution.py:504
  93.5 30.1 %attend.1.made_ref = bf16[1024,2048]{1,0:T(8,128)(2,1)} custom-call(s32[8,128]{1,0:T(8,128)} %get-tuple-element.11.bounds_ref, s32[16,512]{1,0:T(8,128)} %get-tuple-element.12.last_ref, s32[16,512]{1,0:T(8,128)} %get-tuple-element.13.begin_ref, bf16[2,16,512,128]{3,2,1,0:T(8,128)(2,1)} %get-tuple-element.14.turned_ref, ...), custom_call_target="tpu_custom_call" | custom-call | tf_op jit(solution)/shard_map/attend/pallas_call | solution.py:803
  123.6 34.5 %back.1.ret_ref = bf16[8,64,4096]{2,1,0:T(8,128)(2,1)} custom-call(bf16[1024,2048]{1,0:T(8,128)(2,1)} %attend.1.made_ref, s32[1024,128]{1,0:T(8,128)} %get-tuple-element.16.rank_ref), custom_call_target="tpu_custom_call" | custom-call | tf_op jit(solution)/shard_map/back/pallas_call | solution.py:618
  158.1 4.3 %restore.1 = bf16[256,4096]{1,0:T(8,128)(2,1)} custom-call(s32[1]{0:T(128)} %bitcast.cycle_ref, s32[1,256]{1,0:T(1,128)} %bitcast.3, bf16[8,64,4096]{2,1,0:T(8,128)(2,1)} %back.1.ret_ref), custom_call_target="tpu_custom_call" | custom-call | tf_op jit(solution)/shard_map/restore/pallas_call | solution.py:652
